TPU v7x, 32 devices: a whole 2x2x4 slice. The times are simulated.
32 devices in a mesh: section: 2 (over core), dp: 8 (over z, x), rep: 2 (over y).
Axes of the slice: x: 2, y: 2, z: 4, core: 2. Of those that a mesh axis runs over, the one named last changes fastest.
Arguments:
- past_values: bfloat16 [32768, 336], P(('dp', 'rep')), may hold values from -6 to 6
- horizon_label: int32 [32768], P(('dp', 'rep')), may hold values from 0 to 3, as said below
- lookback_observed: int32 [32768, 336], P(('dp', 'rep')), may hold values from 0 to 1, as said below
- prediction_scored: int32 [32768, 64], P(('dp', 'rep')), may hold values from 0 to 1, as said below
- adjoint_prediction: bfloat16 [32768, 64], P(('dp', 'rep')), may hold values from -6 to 6
- adjoint_leftover: bfloat16 [32768, 336], P(('dp', 'rep')), may hold values from -6 to 6
- entry_matrix: bfloat16 [2, 336, 512], P('section'), may hold values from -0.3125 to 0.3125
- inner_matrices: bfloat16 [2, 3, 512, 512], P('section'), may hold values from -0.25 to 0.25
- coefficient_matrices: bfloat16 [2, 2, 512, 512], P('section'), may hold values from -0.25 to 0.25
- lookback_basis: bfloat16 [2, 512, 336], P('section'), may hold values from -0.25 to 0.25
- prediction_basis: bfloat16 [2, 512, 256], P('section'), may hold values from -0.25 to 0.25
- inner_offsets: float32 [2, 6, 512], P('section'), may hold values from -2 to 2
- lookback_offset: float32 [2, 336], P('section'), may hold values from -2 to 2
- prediction_offset: float32 [2, 256], P('section'), may hold values from -2 to 2
Outputs:
- prediction_pair: float32 [2, 32768, 64], P('section', ('dp', 'rep'))
- outcome_pair: float32 [2, 32768, 336], P('section', ('dp', 'rep'))
- grad_first: float32 [2, 336, 512], P('section')
- grad_mid: float32 [2, 3, 512, 512], P('section')
- grad_theta: float32 [2, 2, 512, 512], P('section')
- grad_back: float32 [2, 512, 336], P('section')
- grad_fore: float32 [2, 512, 256], P('section')
- grad_hidden_bias: float32 [2, 6, 512], P('section')
- grad_back_bias: float32 [2, 336], P('section')
- grad_fore_bias: float32 [2, 256], P('section')
Inputs may be any that keep to these rules, and one draw needn't show every extreme that they name: `horizon_label`: group g has horizon 6, 8, 18 or 48 for g = 0, 1, 2, 3. `lookback_observed`: ones only in the last 7 h positions, h the window's horizon. `prediction_scored`: ones only in the first h positions, h the window's horizon.
All inputs are finite; a program needn't handle non-finite values.
Results may differ from a plain program's by a relative error of at most 0.014.
Values may be sent and summed in bfloat16 or wider, within the bound.
A program may use at most 192 MiB of HBM per device.

v0:
```python
import jax
import jax.numpy as jnp
from jax import lax
from jax.sharding import PartitionSpec as P

MICRO = 2


def passed_along(block, axis, distance):
    devices = range(lax.axis_size(axis))
    route = [(i - distance, i) for i in devices if i - distance in devices]
    return lax.ppermute(block, axis, route)


def block_forward(values, look_mask, hor_mask, onehot, weights, offset_vectors):
    first_w, mid_w, theta_w, back_w, fore_w = weights
    hidden_b, back_b, fore_b = offset_vectors
    inside = values * look_mask
    hidden = inside.astype(jnp.bfloat16)
    matrices = [first_w, mid_w[0], mid_w[1], mid_w[2]]
    preacts = []
    layers_out = [hidden]
    for depth in range(4):
        preact = (
            jnp.dot(hidden, matrices[depth], preferred_element_type=jnp.float32) + hidden_b[depth]
        )
        hidden = jax.nn.silu(preact).astype(jnp.bfloat16)
        preacts.append(preact)
        layers_out.append(hidden)
    theta_back = (
        jnp.dot(hidden, theta_w[0], preferred_element_type=jnp.float32) + hidden_b[4]
    ).astype(jnp.bfloat16)
    theta_fore = (
        jnp.dot(hidden, theta_w[1], preferred_element_type=jnp.float32) + hidden_b[5]
    ).astype(jnp.bfloat16)
    backcast = jnp.dot(theta_back, back_w, preferred_element_type=jnp.float32) + back_b
    output_values = jnp.dot(theta_fore, fore_w, preferred_element_type=jnp.float32) + fore_b
    output_values = output_values.reshape(
        output_values.shape[0], onehot.shape[1], hor_mask.shape[1]
    )
    partial_value = jnp.sum(output_values * onehot[:, :, None], axis=1) * hor_mask
    residual = (inside - backcast) * look_mask
    kept = (tuple(layers_out), tuple(preacts), theta_back, theta_fore)
    return (residual, partial_value, kept)


def block_backward(kept, d_resid, prediction_gradient, look_mask, hor_mask, onehot, weights):
    layers_out, preacts, theta_back, theta_fore = kept
    first_w, mid_w, theta_w, back_w, fore_w = weights
    win_rows = d_resid.shape[0]
    direct = d_resid * look_mask
    grad_back = (-direct).astype(jnp.bfloat16)
    grad_heads = (
        (onehot[:, :, None] * (prediction_gradient * hor_mask)[:, None, :])
        .reshape(win_rows, -1)
        .astype(jnp.bfloat16)
    )
    g_back_w = jnp.einsum("nd,nl->dl", theta_back, grad_back, preferred_element_type=jnp.float32)
    g_back_b = jnp.sum(grad_back, axis=0, dtype=jnp.float32)
    g_fore_w = jnp.einsum("nd,nh->dh", theta_fore, grad_heads, preferred_element_type=jnp.float32)
    g_fore_b = jnp.sum(grad_heads, axis=0, dtype=jnp.float32)
    pre_back = jnp.einsum(
        "nl,dl->nd", grad_back, back_w, preferred_element_type=jnp.float32
    ).astype(jnp.bfloat16)
    pre_fore = jnp.einsum(
        "nh,dh->nd", grad_heads, fore_w, preferred_element_type=jnp.float32
    ).astype(jnp.bfloat16)
    top_hidden = layers_out[4]
    g_theta = jnp.stack(
        [
            jnp.einsum("nd,ne->de", top_hidden, pre_back, preferred_element_type=jnp.float32),
            jnp.einsum("nd,ne->de", top_hidden, pre_fore, preferred_element_type=jnp.float32),
        ]
    )
    theta_bias = [
        jnp.sum(pre_back, axis=0, dtype=jnp.float32),
        jnp.sum(pre_fore, axis=0, dtype=jnp.float32),
    ]
    d_hidden = jnp.einsum(
        "ne,de->nd", pre_back, theta_w[0], preferred_element_type=jnp.float32
    ) + jnp.einsum("ne,de->nd", pre_fore, theta_w[1], preferred_element_type=jnp.float32)
    matrices = [first_w, mid_w[0], mid_w[1], mid_w[2]]
    g_mats = [None, None, None, None]
    g_bias = [None, None, None, None]
    for depth in (3, 2, 1, 0):
        sigmoid_z = jax.nn.sigmoid(preacts[depth])
        d_pre = (d_hidden * sigmoid_z * (1.0 + preacts[depth] * (1.0 - sigmoid_z))).astype(
            jnp.bfloat16
        )
        g_mats[depth] = jnp.einsum(
            "nd,ne->de", layers_out[depth], d_pre, preferred_element_type=jnp.float32
        )
        g_bias[depth] = jnp.sum(d_pre, axis=0, dtype=jnp.float32)
        d_hidden = jnp.einsum(
            "ne,de->nd", d_pre, matrices[depth], preferred_element_type=jnp.float32
        )
    d_input = (d_hidden + direct) * look_mask
    gradients = (
        g_mats[0],
        jnp.stack(g_mats[1:]),
        g_theta,
        g_back_w,
        g_fore_w,
        jnp.stack(g_bias + theta_bias),
        g_back_b,
        g_fore_b,
    )
    return (gradients, d_input)


def select_option(leading_segment, items, zero_index, one_index):
    return jnp.where(leading_segment, items[zero_index], items[one_index])


def shards(
    past_values,
    horizon_label,
    lookback_observed,
    prediction_scored,
    adjoint_prediction,
    adjoint_leftover,
    entry_matrix,
    inner_matrices,
    coefficient_matrices,
    lookback_basis,
    prediction_basis,
    inner_offsets,
    lookback_offset,
    prediction_offset,
):
    leading_segment = lax.axis_index("section") == 0
    mb_rows = past_values.shape[0] // MICRO
    horizon_sets = prediction_basis.shape[2] // prediction_scored.shape[1]
    weights = (
        entry_matrix[0],
        inner_matrices[0],
        coefficient_matrices[0],
        lookback_basis[0],
        prediction_basis[0],
    )
    offset_vectors = (inner_offsets[0], lookback_offset[0], prediction_offset[0])

    def segment_sequence(a):
        return [a[m * mb_rows : (m + 1) * mb_rows] for m in range(MICRO)]

    onehot_all = (
        horizon_label[:, None] == jnp.arange(horizon_sets, dtype=jnp.int32)[None, :]
    ).astype(jnp.float32)
    look_parts = segment_sequence(lookback_observed.astype(jnp.float32))
    horizon_shares = segment_sequence(prediction_scored.astype(jnp.float32))
    onehot_parts = segment_sequence(onehot_all)
    input_parts = segment_sequence(past_values.astype(jnp.float32))
    adjoint_prediction_shares = segment_sequence(adjoint_prediction.astype(jnp.float32))
    cot_resid_parts = segment_sequence(adjoint_leftover.astype(jnp.float32))
    width = past_values.shape[1]
    prediction_span = prediction_scored.shape[1]
    received = (
        jnp.zeros((mb_rows, width), jnp.bfloat16),
        jnp.zeros((mb_rows, prediction_span), jnp.bfloat16),
    )
    inputs_seen = []
    kept_list = []
    fore_out = []
    resid_out = []
    for carry_onward in range(MICRO + 1):
        ahead_steps = min(carry_onward, MICRO - 1)
        delay_steps = max(carry_onward - 1, 0)
        look_mask = select_option(leading_segment, look_parts, ahead_steps, delay_steps)
        hor_mask = select_option(leading_segment, horizon_shares, ahead_steps, delay_steps)
        onehot = select_option(leading_segment, onehot_parts, ahead_steps, delay_steps)
        values = jnp.where(
            leading_segment, input_parts[ahead_steps], received[0].astype(jnp.float32)
        )
        residual, partial_value, kept = block_forward(
            values, look_mask, hor_mask, onehot, weights, offset_vectors
        )
        inputs_seen.append(values)
        kept_list.append(kept)
        fore_low = partial_value.astype(jnp.bfloat16)
        fore_out.append(
            jnp.where(
                leading_segment,
                fore_low.astype(jnp.float32),
                received[1].astype(jnp.float32) + partial_value,
            )
        )
        resid_out.append(residual)
        if carry_onward < MICRO:
            received = passed_along((residual.astype(jnp.bfloat16), fore_low), "section", 1)
    cumulative_sums = None
    back_in = jnp.zeros((mb_rows, width), jnp.bfloat16)
    source_derivatives = []
    for carry_onward in range(MICRO + 1):
        ahead_steps = min(carry_onward, MICRO - 1)
        delay_steps = max(carry_onward - 1, 0)
        look_mask = select_option(leading_segment, look_parts, delay_steps, ahead_steps)
        hor_mask = select_option(leading_segment, horizon_shares, delay_steps, ahead_steps)
        onehot = select_option(leading_segment, onehot_parts, delay_steps, ahead_steps)
        prediction_gradient = select_option(
            leading_segment, adjoint_prediction_shares, delay_steps, ahead_steps
        )
        d_resid = jnp.where(
            leading_segment, back_in.astype(jnp.float32), cot_resid_parts[ahead_steps]
        )
        values = jnp.where(
            leading_segment, inputs_seen[delay_steps], inputs_seen[min(carry_onward + 1, MICRO)]
        )
        unused_res, unused_fore, kept = block_forward(
            values, look_mask, hor_mask, onehot, weights, offset_vectors
        )
        gradients, d_input = block_backward(
            kept, d_resid, prediction_gradient, look_mask, hor_mask, onehot, weights
        )
        counted = jnp.where(leading_segment, carry_onward >= 1, carry_onward < MICRO)
        gradients = jax.tree.map(lambda g: jnp.where(counted, g, 0.0), gradients)
        source_derivatives.append(d_input)
        if carry_onward < MICRO:
            back_in = passed_along(d_input.astype(jnp.bfloat16), "section", -1)
        cumulative_sums = (
            gradients
            if cumulative_sums is None
            else jax.tree.map(lambda a, b: a + b, cumulative_sums, gradients)
        )
    cumulative_sums = lax.psum(
        (
            cumulative_sums[0],
            cumulative_sums[1],
            cumulative_sums[2],
            cumulative_sums[3],
            cumulative_sums[4],
            cumulative_sums[5],
            cumulative_sums[6],
            cumulative_sums[7],
        ),
        ("dp", "rep"),
    )
    fore_final = jnp.concatenate(
        [jnp.where(leading_segment, fore_out[m], fore_out[m + 1]) for m in range(MICRO)], axis=0
    )
    ends_final = jnp.concatenate(
        [
            jnp.where(leading_segment, source_derivatives[m + 1], resid_out[m + 1])
            for m in range(MICRO)
        ],
        axis=0,
    )
    return (
        fore_final[None],
        ends_final[None],
        cumulative_sums[0][None],
        cumulative_sums[1][None],
        cumulative_sums[2][None],
        cumulative_sums[3][None],
        cumulative_sums[4][None],
        cumulative_sums[5][None],
        cumulative_sums[6][None],
        cumulative_sums[7][None],
    )


def solution(mesh):
    in_specs = (
        P(("dp", "rep"), None),
        P(("dp", "rep")),
        P(("dp", "rep"), None),
        P(("dp", "rep"), None),
        P(("dp", "rep"), None),
        P(("dp", "rep"), None),
        P("section", None, None),
        P("section", None, None, None),
        P("section", None, None, None),
        P("section", None, None),
        P("section", None, None),
        P("section", None, None),
        P("section", None),
        P("section", None),
    )
    out_specs = (
        P("section", ("dp", "rep"), None),
        P("section", ("dp", "rep"), None),
        P("section", None, None),
        P("section", None, None, None),
        P("section", None, None, None),
        P("section", None, None),
        P("section", None, None),
        P("section", None, None),
        P("section", None),
        P("section", None),
    )
    return jax.shard_map(shards, mesh=mesh, in_specs=in_specs, out_specs=out_specs, check_vma=False)
```

profile of v0, /device:TPU:0, one launch (start us, length us, event | category | flops | bytes accessed | tf_op | source)
XLA Modules:
  0.0 461.0 jit_solution(5319460242039114331)
XLA Ops:
  12.2 4.2 multiply_convert_fusion.34
  16.4 4.2 multiply_convert_fusion.32
  20.5 3.9 fusion.21
  24.5 3.2 collective-permute-start
  32.6 3.4 fusion.24
  36.0 4.6 multiply_convert_fusion.30
  40.5 4.2 multiply_convert_fusion.28
  44.7 4.6 fusion.233
  56.6 3.5 convert_reduce_fusion.20
  85.7 3.3 multiply_convert_fusion
  89.0 3.7 fusion.37
  92.8 3.5 convolution_select_fusion.1
  96.2 3.4 convolution_bitcast_fusion.4
  101.4 4.5 multiply_convert_fusion.26
  105.8 4.2 multiply_convert_fusion.24
  110.0 3.4 fusion.22
  123.3 3.8 fusion.33
  127.0 3.2 convolution_bitcast_fusion.2
  130.3 4.1 fusion.36
  134.4 3.4 convolution_bitcast_fusion
  156.2 3.1 broadcast_select_fusion
  165.5 3.5 convolution_select_fusion
  190.7 3.9 fusion.26
  194.6 3.4 fusion.29
  198.0 4.4 fusion.5
  203.0 3.4 fusion.2
  208.9 4.0 collective-permute-start.1
  213.0 3.4 fusion.23
  226.2 4.3 fusion.14
  230.7 80.2 %all-reduce = (f32[1,6,512]{2,0,1:T(1,128)}, f32[1,336]{1,0:T(1,128)}, f32[1,256]{1,0:T(1,128)}) all-reduce(f32[1,6,512]{2,0,1:T(1,128)S(1)} %broadcast_in_dim.102, f32[1,336]{1,0:T(1,128)S(1)} %broadcast_in_dim.104, f32[1,256]{1,0:T(1,128)S(1)} %broadcast_in_dim.106), channel_id=1, replica_groups=mesh['section'=2,'dp'=8,'rep'=2] {'dp','rep'}, use_global_device_ids=true, to_apply=%region_26.27 | all-reduce | flops 3664 | bytes 29312 | tf_op jit(solution)/shard_map/psum | solution.py:224
  315.2 129.2 %all-reduce.4.cloned.1.call-done = (f32[1,336,512]{2,1,0:T(8,128)}, f32[1,3,512,512]{3,2,1,0:T(8,128)}, f32[1,2,512,512]{3,2,1,0:T(8,128)}, f32[1,512,336]{1,2,0:T(8,128)}, f32[1,512,256]{2,1,0:T(8,128)}) async-done(((f32[1,336,512]{2,1,0:T(8,128)}, f32[1,3,512,512]{3,2,1,0:T(8,128)}, f32[1,2,512,512]{3,2,1,0:T(8,128)}, f32[1,512,336]{1,2,0:T(8,128)}, f32[1,512,256]{2,1,0:T(8,128)}), ...) | async-done | bytes 7143440 | tf_op jit(solution)/shard_map/psum | solution.py:224
  446.5 4.0 copy.32
  (298 shorter events, 122.7 us)
Async XLA Ops:
  7.2 5.0 %copy-start = (bf16[1,336,512]{2,1,0:T(8,128)(2,1)S(1)}, bf16[1,336,512]{2,1,0:T(8,128)(2,1)}, u32[]{:S(2)}) copy-start(bf16[1,336,512]{2,1,0:T(8,128)(2,1)} %param.20) | copy-start | bytes 1032196
  7.2 437.3 %all-reduce.4.cloned.1.call-start = ((), (), s32[]{:S(2)}) async-start(), calls=%async_computation | async-start | bytes 14286848 | tf_op jit(solution)/shard_map/psum | solution.py:224
  8.0 182.6 %copy-start.76 = (f32[1,1,512]{2,0,1:T(1,128)}, f32[1,1,512]{2,0,1:T(1,128)S(1)}, u32[]{:S(2)}) copy-start(f32[1,1,512]{2,0,1:T(1,128)S(1)} %get-tuple-element.49) | copy-start | bytes 6148
  12.2 32.6 %copy-start.77 = (f32[336]{0:T(512)}, f32[336]{0:T(512)S(1)}, u32[]{:S(2)}) copy-start(f32[336]{0:T(512)S(1)} %reduce.3) | copy-start | bytes 4036
  20.5 7.2 %copy-start.59 = (s32[2048]{0:T(1024)S(1)}, s32[2048]{0:T(1024)}, u32[]{:S(2)}) copy-start(s32[2048]{0:T(1024)} %param.15) | copy-start | bytes 24580
  20.5 8.4 %copy-start.56 = (bf16[2048,64]{0,1:T(8,128)(2,1)S(1)}, bf16[2048,64]{0,1:T(8,128)(2,1)}, u32[]{:S(2)}) copy-start(bf16[2048,64]{0,1:T(8,128)(2,1)} %param.18) | copy-start | bytes 786436
  24.5 11.5 %collective-permute-start = (bf16[1024,336]{0,1:T(8,128)(2,1)}, bf16[1024,336]{0,1:T(8,128)(2,1)}, u32[]{:S(2)}, u32[]{:S(2)}) collective-permute-start(bf16[1024,336]{0,1:T(8,128)(2,1)} %fusion.21), channel_id=1, source_target_pairs={{0,16},{1,17},{2,18},{3,19},{4,20},{5,21},{6,22},{7,23},{8,24},{9,... | collective-permute-start | bytes 2064392 | tf_op jit(solution)/shard_map/ppermute | solution.py:12
  49.3 7.2 %collective-permute-start.2 = (bf16[1024,336]{0,1:T(8,128)(2,1)}, bf16[1024,336]{0,1:T(8,128)(2,1)S(1)}, u32[]{:S(2)}, u32[]{:S(2)}) collective-permute-start(bf16[1024,336]{0,1:T(8,128)(2,1)} %get-tuple-element.58), channel_id=1, source_target_pairs={{0,16},{1,17},{2,18},{3,19},{4,20},{5,21},{6,22},{7,23},{8,24},{9,... | collective-permute-start | bytes 2064392 | tf_op jit(solution)/shard_map/ppermute | solution.py:12
  50.9 5.7 %copy-start.4 = (f32[2048,336]{0,1:T(8,128)S(1)}, f32[2048,336]{0,1:T(8,128)}, u32[]{:S(2)}) copy-start(f32[2048,336]{0,1:T(8,128)} %convert_element_type.375) | copy-start | bytes 8257540
  56.5 10.9 %copy-start.49 = (bf16[1024,512]{1,0:T(8,128)(2,1)}, bf16[1024,512]{1,0:T(8,128)(2,1)S(1)}, u32[]{:S(2)}) copy-start(bf16[1024,512]{1,0:T(8,128)(2,1)S(1)} %get-tuple-element.97) | copy-start | bytes 3145732
  60.1 17.4 %copy-start.6 = (bf16[1024,336]{0,1:T(8,128)(2,1)}, bf16[1024,336]{0,1:T(8,128)(2,1)S(1)}, u32[]{:S(2)}) copy-start(bf16[1024,336]{0,1:T(8,128)(2,1)S(1)} %get-tuple-element.33) | copy-start | bytes 2064388
  60.1 20.9 %copy-start.11 = (bf16[1024,336]{0,1:T(8,128)(2,1)}, bf16[1024,336]{0,1:T(8,128)(2,1)S(1)}, u32[]{:S(2)}) copy-start(bf16[1024,336]{0,1:T(8,128)(2,1)S(1)} %get-tuple-element.34) | copy-start | bytes 2064388
  61.6 4.6 copy-start.44
  121.8 17.7 %collective-permute-start.4 = (bf16[1024,336]{0,1:T(8,128)(2,1)}, bf16[1024,336]{0,1:T(8,128)(2,1)}, u32[]{:S(2)}, u32[]{:S(2)}) collective-permute-start(bf16[1024,336]{0,1:T(8,128)(2,1)} %fusion.20), channel_id=1, source_target_pairs={{16,0},{17,1},{18,2},{19,3},{20,4},{21,5},{22,6},{23,7},{24,8},{25... | collective-permute-start | bytes 2064392 | tf_op jit(solution)/shard_map/ppermute | solution.py:12
  156.2 4.6 copy-start.86
  159.3 5.0 %collective-permute-start.5 = (bf16[1024,336]{0,1:T(8,128)(2,1)S(1)}, bf16[1024,336]{0,1:T(8,128)(2,1)S(1)}, u32[]{:S(2)}, u32[]{:S(2)}) collective-permute-start(bf16[1024,336]{0,1:T(8,128)(2,1)S(1)} %get-tuple-element.37), channel_id=1, source_target_pairs={{16,0},{17,1},{18,2},{19,3},{20,4},{21,5},{22,6},{23,7},{24,8},{25... | collective-permute-start | bytes 2064392 | tf_op jit(solution)/shard_map/ppermute | solution.py:12
  198.0 4.5 copy-start.34
  198.0 4.9 %copy-start.46 = (f32[1,512,512]{2,1,0:T(8,128)S(1)}, f32[1,512,512]{2,1,0:T(8,128)}, u32[]{:S(2)}) copy-start(f32[1,512,512]{2,1,0:T(8,128)} %convolution_bitcast_fusion.7) | copy-start | bytes 3145732
  206.3 6.6 %copy-start.85 = (f32[1,256]{1,0:T(1,128)S(1)}, f32[1,256]{1,0:T(1,128)}, u32[]{:S(2)}) copy-start(f32[1,256]{1,0:T(1,128)} %param.27) | copy-start | bytes 3076
  208.9 7.5 %copy-start.57 = (f32[1024,4]{0,1:T(4,128)S(1)}, f32[1024,4]{0,1:T(4,128)}, u32[]{:S(2)}) copy-start(f32[1024,4]{0,1:T(4,128)} %get-tuple-element.48) | copy-start | bytes 49156
  208.9 8.9 %collective-permute-start.1 = (bf16[1024,64]{0,1:T(8,128)(2,1)}, bf16[1024,64]{0,1:T(8,128)(2,1)S(1)}, u32[]{:S(2)}, u32[]{:S(2)}) collective-permute-start(bf16[1024,64]{0,1:T(8,128)(2,1)} %fusion.162), channel_id=1, source_target_pairs={{0,16},{1,17},{2,18},{3,19},{4,20},{5,21},{6,22},{7,23},{8,24},{9,... | collective-permute-start | bytes 393224 | tf_op jit(solution)/shard_map/ppermute | solution.py:12
  216.4 5.7 %copy-start.62 = (f32[4,64]{1,0:T(4,128)S(1)}, f32[4,64]{1,0:T(4,128)}, u32[]{:S(2)}) copy-start(f32[4,64]{1,0:T(4,128)} %get-tuple-element.41) | copy-start | bytes 3076
  216.4 5.7 %copy-start.63 = (f32[4,64]{1,0:T(4,128)S(1)}, f32[4,64]{1,0:T(4,128)}, u32[]{:S(2)}) copy-start(f32[4,64]{1,0:T(4,128)} %get-tuple-element.100) | copy-start | bytes 3076
  216.4 5.8 %copy-start.61 = (f32[512]{0:T(512)S(1)}, f32[512]{0:T(512)}, u32[]{:S(2)}) copy-start(f32[512]{0:T(512)} %get-tuple-element.96) | copy-start | bytes 6148
  216.4 5.8 %copy-start.64 = (f32[512]{0:T(512)S(1)}, f32[512]{0:T(512)}, u32[]{:S(2)}) copy-start(f32[512]{0:T(512)} %get-tuple-element.94) | copy-start | bytes 6148
  216.4 5.8 %copy-start.65 = (f32[512]{0:T(512)S(1)}, f32[512]{0:T(512)}, u32[]{:S(2)}) copy-start(f32[512]{0:T(512)} %get-tuple-element.92) | copy-start | bytes 6148
  216.4 5.8 %copy-start.66 = (f32[512]{0:T(512)S(1)}, f32[512]{0:T(512)}, u32[]{:S(2)}) copy-start(f32[512]{0:T(512)} %get-tuple-element.90) | copy-start | bytes 6148
  216.4 5.8 %copy-start.67 = (f32[512]{0:T(512)S(1)}, f32[512]{0:T(512)}, u32[]{:S(2)}) copy-start(f32[512]{0:T(512)} %get-tuple-element.88) | copy-start | bytes 6148
  220.4 2.6 collective-permute-start.3
  226.1 4.5 copy-start.71
  226.1 4.5 copy-start.72
  226.1 4.5 copy-start.73
  (77 other events, 200.4 us)
Sparse Core Ops, SparseCore 0:
  206.5 237.9 all-reduce.3
where the time goes:
time: 470 us; the launch traced here: 461 us
  matrix products  163 us (35%)
  waiting for transfers between devices  129 us (27%)
  blocking collectives  80.2 us (17%)
  other arithmetic  37.4 us (8%)
  local copies, waits for them, and re-layouts  21.9 us (5%)
  between operations  15.3 us (3%)
  starting transfers between devices  13.4 us (3%)
    psum x1, waiting for transfers between devices, shards(): lax.psum((cumulative_sums[0], cumulative_sums[1], cumulative_sums[2], cum...  129 us
    psum x1, blocking collectives, shards(): lax.psum((cumulative_sums[0], cumulative_sums[1], cumulative_sums[2], cum...  80.2 us
    dot_general x18, matrix products, block_forward(): jnp.dot(hidden, matrices[depth], preferred_element_type=jnp.float32)  37.6 us
    dot_general x12, matrix products, block_backward(): jnp.einsum('ne,de->nd', d_pre, matrices[depth], preferred_element_type=jn...  26.4 us
    dot_general x12, matrix products, block_backward(): jnp.einsum('nd,ne->de', layers_out[depth], d_pre, preferred_element_type=...  22.1 us
    unnamed x209, local copies, waits for them, and re-layouts  20.3 us
    ppermute x6, starting transfers between devices, passed_along(): return lax.ppermute(block, axis, route)  13.3 us
    dot_general x3, matrix products, block_forward(): jnp.dot(theta_back, back_w, preferred_element_type=jnp.float32) + back_b  12.8 us
  transfers between devices with their start and end apart: 7, of which 2 were waited for; matrix products, arithmetic and copies ran while one was open for 12% of the time, Pallas kernels for 0%

commit v1 on v0

v1 whole, which is shorter than its diff:
```python
import functools
from typing import Any, NamedTuple

import jax
import jax.numpy as jnp
from jax import lax
from jax.experimental import pallas as pl
from jax.experimental.pallas import tpu as pltpu
from jax.sharding import PartitionSpec as P

BF16 = jnp.bfloat16
F32 = jnp.float32
MESH = pl.DeviceIdType.MESH

BACK, FORE, TB, TF, M0, M1, M2, FIRST = range(8)
PIECE_ROWS = (384, 256, 512, 512, 512, 512, 512, 384)
ROUNDS = (
    (0, (TF,)),
    (1, (TB, TF)),
    (1, (M2,)),
    (1, (M1,)),
    (1, (M0,)),
    (1, (FIRST,)),
    (1, (BACK, FORE)),
    (0, (BACK, FORE, TB)),
    (0, (M2,)),
    (0, (M1,)),
    (0, (M0,)),
    (0, (FIRST,)),
)
D2D, S1, S2, S3, S4, G3, G2, G1, G1X, GD = range(10)
LANDING = (1, 2, 4, 8, 8)
(
    LOAD, Z1_0, Z2_0, Z3_0, Z4_0, GH_0, GTF_0, BACK_0, Z1_1, Z2_1, Z3_1, Z4_1, PP_1, GT_1, DH4_1,
    B3_1, B2_1, B1_1, B0_1, GB_0, GTB_0, DH4_0, B3_0, B2_0, B1_0, B0_0, HEADS_0, THETA_1, FINAL_1,
) = range(29)
STEP = 1000
ORDER = (
    LOAD, Z1_0, Z2_0, Z3_0, Z4_0, GH_0, GTF_0, BACK_0, Z1_1, 1000, Z2_1, Z3_1, Z4_1, PP_1, GT_1, 1001, DH4_1,
    B3_1, 1010, B2_1, 1002, 1020, B1_1, 1030, B0_1, 1040, GB_0, 1003, 1011, 1050, 1021, HEADS_0, 1031, GTB_0,
    1041, DH4_0, 1004, 1051, 1070, B3_0, 1012, B2_0, 1005, 1022, 1032, 1080, B1_0, 1042, 1052, 1071, 1090,
    1013, 1023, B0_0, 1006, 1033, 1043, 1053, 1081, 1100, 1110, THETA_1, 1072, 1007, 1091, FINAL_1, 1060,
    1014, 1101, 1111, 1024, 1034, 1073, 1044, 1054, 1082, 1092, 1061, 1015, 1102, 1025, 1035, 1045, 1055,
    1112, 1083, 1093, 1103, 1074, 1062, 1113, 1016, 1075, 1063, 1026, 1036, 1046, 1056, 1017, 1027, 1084,
    1094, 1037, 1104, 1114, 1047, 1057, 1076, 1085, 1095, 1105, 1115, 1064, 1086, 1096, 1077, 1065, 1106,
    1116, 1087, 1097, 1066, 1107, 1117, 1067,
)


def rows_of(number):
    return sum(PIECE_ROWS[piece] for piece in ROUNDS[number][1])


def place_of(block, piece):
    for number, (at, pieces) in enumerate(ROUNDS):
        if at == block and piece in pieces:
            return number, sum(PIECE_ROWS[p] for p in pieces[: pieces.index(piece)])


def nn(a, b):
    return jnp.dot(a, b, preferred_element_type=F32)


def nt(a, b):
    return lax.dot_general(a, b, (((1,), (1,)), ((), ())), preferred_element_type=F32)


def tn(a, b):
    return lax.dot_general(a, b, (((0,), (0,)), ((), ())), preferred_element_type=F32)


class Inputs(NamedTuple):
    past: Any
    look: Any
    label: Any
    scored: Any
    adjp: Any
    adjl: Any


class Given(NamedTuple):
    first: Any
    mid: Any
    theta: Any
    back: Any
    fore: Any
    hid: Any
    backb: Any
    foreb: Any


class Results(NamedTuple):
    pair: Any
    outcome: Any
    first: Any
    mid: Any
    theta: Any
    back: Any
    fore: Any


class Weights(NamedTuple):
    first: Any
    hid: Any
    mid0: Any
    mid1: Any
    mid2: Any
    theta_b: Any
    theta_f: Any
    back: Any
    backb: Any
    fore: Any
    foreb: Any


class Block(NamedTuple):
    h: Any
    d: Any
    gb: Any
    pp: Any
    bias: Any
    hid: Any
    backb: Any
    foreb: Any


class Round(NamedTuple):
    part: Any
    landing: Any
    rest: Any


class Scratch(NamedTuple):
    weights: Any
    blocks: Any
    rounds: Any
    observed: Any
    mask: Any
    label: Any
    scored: Any
    adjp: Any
    gh: Any
    tt: Any
    sent: Any
    total: Any
    dinput: Any
    r2: Any
    load_sem: Any
    weight_sem: Any
    weight_send: Any
    send_sem: Any
    recv_sem: Any
    out_sem: Any
    give_send: Any
    give_recv: Any


def scratch(n):
    def weights():
        square = pltpu.VMEM((512, 512), BF16)
        return Weights(
            first=pltpu.VMEM((336, 512), BF16),
            hid=pltpu.VMEM((24, 128), F32),
            mid0=square,
            mid1=square,
            mid2=square,
            theta_b=square,
            theta_f=square,
            back=pltpu.VMEM((336, 512), BF16),
            backb=pltpu.VMEM((1, 336), F32),
            fore=pltpu.VMEM((512, 256), BF16),
            foreb=pltpu.VMEM((1, 256), F32),
        )

    def block():
        return Block(
            h=[pltpu.VMEM(((336 if k == 0 else 512) + 16, n), BF16) for k in range(5)],
            d=[pltpu.VMEM((512, n), BF16) for _ in range(4)],
            gb=pltpu.VMEM((336, n), BF16),
            pp=pltpu.VMEM((1024, n), BF16),
            bias=pltpu.VMEM((16, 512), F32),
            hid=pltpu.VMEM((512, 8), F32),
            backb=pltpu.VMEM((336, 8), F32),
            foreb=pltpu.VMEM((256, 8), F32),
        )

    def a_round(number):
        rows = rows_of(number)
        half = rows // 2

        def landing(portion):
            shape = (half // portion, 512)
            return pltpu.VMEM(shape if shape[0] % 16 == 0 else (2 * shape[0], 256), BF16)

        return Round(
            part=pltpu.VMEM((rows, 512), BF16),
            landing=[landing(portion) for portion in LANDING],
            rest=pltpu.VMEM((half, 512), BF16),
        )

    dma = pltpu.SemaphoreType.DMA
    count = len(ROUNDS)
    return Scratch(
        weights=[weights(), weights()],
        blocks=[block(), block()],
        rounds=[a_round(number) for number in range(count)],
        observed=pltpu.VMEM((336, n), jnp.int32),
        mask=pltpu.VMEM((336, n), BF16),
        label=pltpu.VMEM((n // 128, 128), jnp.int32),
        scored=pltpu.VMEM((64, n), jnp.int32),
        adjp=pltpu.VMEM((64, n), BF16),
        gh=pltpu.VMEM((256, n), BF16),
        tt=pltpu.VMEM((1024, n), BF16),
        sent=pltpu.VMEM((64, n), BF16),
        total=pltpu.VMEM((64, n), BF16),
        dinput=pltpu.VMEM((336, n), BF16),
        r2=pltpu.VMEM((336, n), BF16),
        load_sem=dma((6,)),
        weight_sem=dma((2, 11)),
        weight_send=dma((2, 11)),
        send_sem=dma((count, 10)),
        recv_sem=dma((count, 10)),
        out_sem=dma((2 * 8, 4)),
        give_send=dma((4,)),
        give_recv=dma((4,)),
    )


def body(n, whole, treedef, *refs):
    inputs, given, outs, s = jax.tree.unflatten(treedef, refs)
    weights, blocks, rounds = s.weights, s.blocks, s.rounds

    c = lax.axis_index("section")
    dp = lax.axis_index("dp")
    y = lax.axis_index("rep")
    z = lax.div(dp, 2)
    x = lax.rem(dp, 2)
    other = 1 - c
    dpx = dp + 1 - 2 * x
    dpz = dp + 2 - 4 * lax.rem(z, 2)
    dpm = 2 * (3 - z) + x
    ry = 1 - y
    dp1 = jnp.where(c == 0, dpx, dp)
    rep1 = jnp.where(c == 0, y, ry)
    dp2 = jnp.where(c == 0, dp, dpx)
    rep2 = jnp.where(c == 0, ry, y)
    bits = (jnp.where(c == 0, x, y), lax.rem(lax.div(z + 1, 2), 2), jnp.where(c == 0, y, x))

    mine = pl.ds(pl.multiple_of(c * n, 128), n)
    label_rows = n // 128
    loads = Inputs(
        past=(inputs.past.at[:, mine], blocks[0].h[0].at[pl.ds(0, 336)]),
        look=(inputs.look.at[:, mine], s.observed),
        label=(inputs.label.at[pl.ds(pl.multiple_of(c * label_rows, 8), label_rows)], s.label),
        scored=(inputs.scored.at[:, mine], s.scored),
        adjp=(inputs.adjp.at[:, mine], s.adjp),
        adjl=(inputs.adjl.at[:, mine], blocks[1].gb),
    )
    loads = Inputs(*(pltpu.make_async_copy(*pair, s.load_sem.at[i]) for i, pair in enumerate(loads)))
    sources = Weights(
        first=given.first.at[0],
        hid=given.hid,
        mid0=given.mid.at[0, 0],
        mid1=given.mid.at[0, 1],
        mid2=given.mid.at[0, 2],
        theta_b=given.theta.at[0, 0],
        theta_f=given.theta.at[0, 1],
        back=given.back,
        backb=given.backb,
        fore=given.fore.at[0],
        foreb=given.foreb,
    )

    def weight_local(block, i):
        return pltpu.make_async_copy(sources[i], weights[block][i], s.weight_sem.at[block, i])

    def weight_remote(block, i):
        return pltpu.make_async_remote_copy(
            sources[i],
            weights[block][i],
            s.weight_send.at[block, i],
            s.weight_sem.at[block, i],
            device_id=(other, dp, y),
            device_id_type=MESH,
        )

    names = Weights(*range(11))

    waited = set()

    def wait_weights(block, *keys):
        for key in keys:
            if (block, key) not in waited:
                waited.add((block, key))
                weight_local(block, key).wait()

    def regions(number, base):
        n1 = rows_of(number) // 4

        def at(start, count, col=0, width=512):
            if width == 512:
                return (pl.ds(pl.multiple_of(start, 16), count), slice(None))
            return (pl.ds(pl.multiple_of(start, 16), count), pl.ds(pl.multiple_of(col, 128), width))

        start1 = base + bits[0] * n1
        start2 = start1 + bits[1] * (n1 // 2)
        keep = [at(base, 2 * n1), at(start1, n1), at(start2, n1 // 2)]
        give = [None, at(base + (1 - bits[0]) * n1, n1), at(start1 + (1 - bits[1]) * (n1 // 2), n1 // 2)]
        n3 = n1 // 4
        if n3 % 16 == 0:
            keep.append(at(start2 + bits[2] * n3, n3))
            give.append(at(start2 + (1 - bits[2]) * n3, n3))
        else:
            keep.append(at(start2, n1 // 2, bits[2] * 256, 256))
            give.append(at(start2, n1 // 2, (1 - bits[2]) * 256, 256))
        return keep, give

    def summed(number):
        return regions(number, c * (rows_of(number) // 2))

    def message(number, kind):
        r = rounds[number]
        half = rows_of(number) // 2
        device = (
            (other, dp, y),
            (c, dp1, rep1),
            (c, dpz, y),
            (c, dp2, rep2),
            (c, dpm, y),
            (c, dp2, rep2),
            (c, dpz, y),
            (c, dp1, rep1),
            (other, dp1, rep1),
            (other, dp, y),
        )[kind]
        if kind <= S4:
            keep, give = summed(number)
            where = (
                (pl.ds(pl.multiple_of(other * half, 16), half), slice(None)),
                give[1],
                give[2],
                give[3],
                keep[3],
            )[kind]
            src, dst = r.part.at[where], r.landing[kind]
        else:
            keep, _ = regions(number, 0)
            where = keep[(3, 2, 1, 1, 1 if whole else 0)[kind - G3]]
            src = r.landing[D2D].at[where]
            dst = src if kind <= G1 else r.rest.at[where]
        return pltpu.make_async_remote_copy(
            src,
            dst,
            s.send_sem.at[number, kind],
            s.recv_sem.at[number, kind],
            device_id=device,
            device_id_type=MESH,
        )

    def fold(number, kind, where, *buffer):
        part = rounds[number].part
        part[where] = part[where] + rounds[number].landing[kind][buffer]

    def fold_and_send(number, kind):
        keep, give = summed(number)
        level = kind + 1
        bit = bits[kind]
        rows, cols = rounds[number].landing[kind].shape

        def of_landing(side):
            if rows // 2 % 16 == 0:
                return (pl.ds(pl.multiple_of(side * (rows // 2), 16), rows // 2), slice(None))
            return (slice(None), pl.ds(pl.multiple_of(side * (cols // 2), 128), cols // 2))

        fold(number, kind, give[level], *of_landing(1 - bit))
        message(number, level).start()
        fold(number, kind, keep[level], *of_landing(bit))

    def settle(number, kind, level):
        r = rounds[number]
        here = regions(number, 0)[0][level]
        r.landing[D2D][here] = r.part[summed(number)[0][level]] + r.landing[kind][...]

    def deliver(number):
        block, pieces = ROUNDS[number]
        half = rows_of(number) // 2
        copies = []
        first = 0
        for piece in pieces:
            count = (336, 256, 512, 512, 512, 512, 512, 352)[piece]
            out = (outs.back, None, outs.theta.at[0], outs.theta.at[1], *(outs.mid.at[k] for k in range(3)), outs.first)
            used = 0
            for side in range(2):
                low, high = max(first, side * half), min(first + count, (side + 1) * half)
                if low >= high:
                    continue
                held = rounds[number].landing[D2D] if side == block else rounds[number].rest
                src = held.at[pl.ds(low - side * half, high - low)]
                if piece == FORE:
                    ways = [
                        (src.at[:, pl.ds(256 * k, 256)], outs.fore.at[pl.ds(256 * k + low - first, high - low)])
                        for k in range(2)
                    ]
                else:
                    ways = [(src, out[piece].at[pl.ds(low - first, high - low)])]
                for way in ways:
                    copies.append(pltpu.make_async_copy(*way, s.out_sem.at[8 * block + piece, used]))
                    used += 1
            first += PIECE_ROWS[piece]
        return copies

    def chip_step(number):
        block = ROUNDS[number][0]
        message(number, D2D).wait_recv()
        settle_half(number)
        pl.when(c != block)(lambda: message(number, GD).start())

        @pl.when(c == block)
        def _():
            message(number, GD).wait_recv()
            for copy in deliver(number):
                copy.start()

    def settle_half(number):
        r = rounds[number]
        r.landing[D2D][...] = r.landing[D2D][...] + r.part[summed(number)[0][0]]

    def step(number, kind):
        block = ROUNDS[number][0]
        if kind < G1:
            message(number, kind).wait_recv()
        if kind < S3:
            fold_and_send(number, kind)
        elif kind == S3:
            fold(number, kind, summed(number)[0][3], ...)
            message(number, S4).start()
        elif kind == S4:
            settle(number, kind, 3)
            message(number, G3).start()
        elif kind == G3:
            message(number, G2).start()
        elif kind == G2:
            pl.when(c == block)(lambda: message(number, G1).start())

            @pl.when(c != block)
            def _():
                message(number, G1X).start()
                message(number, GD).start()
        else:

            @pl.when(c == block)
            def _():
                quarter = rows_of(number) // 4
                for kind, ref, side in (
                    (G1, rounds[number].landing[D2D], 1 - bits[0]),
                    (GD, rounds[number].rest, bits[2]),
                    (G1X, rounds[number].rest, 1 - bits[2]),
                ):
                    ref = ref.at[pl.ds(pl.multiple_of(side * quarter, 16), quarter)]
                    pltpu.make_async_remote_copy(
                        ref,
                        ref,
                        s.send_sem.at[number, kind],
                        s.recv_sem.at[number, kind],
                        device_id=(other, dp, y),
                        device_id_type=MESH,
                    ).wait_recv()
                for copy in deliver(number):
                    copy.start()

    def wait_sends():
        for number, (block, _) in enumerate(ROUNDS):
            for kind in (D2D, S1, S2, S3, S4, G3, G2) if whole else (D2D,):
                message(number, kind).wait_send()
            if whole:
                pl.when(c == block)(lambda number=number: message(number, G1).wait_send())
                pl.when(c != block)(lambda number=number: message(number, G1X).wait_send())
            pl.when(c != block)(lambda number=number: message(number, GD).wait_send())

    def result(i):
        src = (s.sent, s.total, s.dinput, s.r2)[i]
        dst = (outs.pair, outs.outcome)[i // 2].at[:, mine]
        local = pltpu.make_async_copy(src, dst, s.give_send.at[i])
        remote = pltpu.make_async_remote_copy(
            src, dst, s.give_send.at[i], s.give_recv.at[i], device_id=(other, dp, y), device_id_type=MESH
        )
        return i % 2, local, remote

    def hand_over(i):
        keeper, local, remote = result(i)
        pl.when(c == keeper)(lambda: local.start())
        pl.when(c != keeper)(lambda: remote.start())

    def handed_over():
        for i in range(4):
            keeper, local, remote = result(i)

            @pl.when(c == keeper)
            def _(local=local, remote=remote):
                local.wait()
                remote.wait_recv()

            pl.when(c != keeper)(lambda remote=remote: remote.wait_send())

    missing = [set(pieces) for _, pieces in ROUNDS]

    def store(block, piece, value):
        number, first = place_of(block, piece)
        missing[number].discard(piece)
        value = value.astype(BF16)
        part = rounds[number].part
        if piece == FORE:
            for k in range(2):
                part[first : first + 256, 256 * k : 256 * (k + 1)] = value[256 * k : 256 * (k + 1)]
        else:
            part[first : first + value.shape[0], :] = value

    def store_with_bias(block, piece, value, row):
        k = value.shape[0] - 16
        blocks[block].bias[row : row + 1, :] = value[k : k + 1]
        store(block, piece, value[:k])

    def row_sums(block, row, value):
        folded = value[:, 0:128]
        for i in range(1, n // 128):
            folded = folded + value[:, 128 * i : 128 * (i + 1)]
        sums = nt(jnp.ones((16, 128), BF16), folded.astype(BF16))
        blocks[block].bias[row : row + 1, 0 : value.shape[0]] = sums[0:1]

    def layer(block, depth):
        b, w = blocks[block], weights[block]
        h = b.h[depth - 1]
        zed = tn(w[(names.first, names.mid0, names.mid1, names.mid2)[depth - 1]][...], h[0 : h.shape[0] - 16, :])
        zed = zed + b.hid[:, depth - 1 : depth]
        sig = 0.5 * jnp.tanh(0.5 * zed) + 0.5
        out = zed * sig
        b.h[depth][0:512, :] = out.astype(BF16)
        b.d[depth - 1][...] = (sig + out * (1.0 - sig)).astype(BF16)

    def theta(block, k):
        w = weights[block][names.theta_b + k]
        return (tn(w[...], blocks[block].h[4][0:512, :]) + blocks[block].hid[:, 4 + k : 5 + k]).astype(BF16)

    def heads(block, theta_f):
        wide = tn(weights[block].fore[...], theta_f) + blocks[block].foreb[:, 0:1]
        row = label_row()
        chosen = jnp.zeros((64, n), F32)
        for g in range(4):
            chosen = chosen + jnp.where(row == g, wide[64 * g : 64 * (g + 1)], 0.0)
        return chosen * s.scored[...].astype(F32)

    def residual(block, theta_b):
        backcast = nn(weights[block].back[...], theta_b) + blocks[block].backb[:, 0:1]
        return (blocks[block].h[0][0:336, :].astype(F32) - backcast) * s.mask[...].astype(F32)

    def inward(block, depth, dh):
        d = blocks[block].d[depth - 1]
        d[...] = (dh * d[...].astype(F32)).astype(BF16)

    def layer_biases(block):
        b, w = blocks[block], weights[block]
        lines = [
            jnp.concatenate([w.hid[4 * k + i : 4 * k + i + 1, :] for i in range(4)], axis=1) for k in range(6)
        ]
        lines.append(jnp.zeros((2, 512), F32))
        b.hid[...] = jnp.concatenate(lines, axis=0).T

    def end_biases(block):
        b, w = blocks[block], weights[block]
        wait_weights(block, names.backb, names.foreb)
        b.backb[...] = jnp.broadcast_to(w.backb[...], (8, 336)).T
        b.foreb[...] = jnp.broadcast_to(w.foreb[...], (8, 256)).T

    def label_row():
        return jnp.concatenate([s.label[i : i + 1, :] for i in range(label_rows)], axis=1)

    def run(task):
        one, two = blocks
        if task == LOAD:
            loads.look.wait()
            mask = s.observed[...].astype(F32).astype(BF16)
            s.mask[...] = mask
            loads.past.wait()
            one.h[0][0:336, :] = one.h[0][0:336, :] * mask
            for b in blocks:
                for h in b.h:
                    k = h.shape[0] - 16
                    h[k : k + 16, :] = jnp.ones((16, n), BF16)
                b.bias[...] = jnp.zeros((16, 512), F32)
            wait_weights(0, names.hid)
            layer_biases(0)
        elif task in (Z1_0, Z2_0, Z3_0, Z4_0):
            depth = task - Z1_0 + 1
            wait_weights(0, (names.first, names.mid0, names.mid1, names.mid2)[depth - 1])
            layer(0, depth)
        elif task in (Z1_1, Z2_1, Z3_1, Z4_1):
            depth = task - Z1_1 + 1
            if depth == 1:
                wait_weights(1, names.hid)
                layer_biases(1)
            wait_weights(1, (names.first, names.mid0, names.mid1, names.mid2)[depth - 1])
            layer(1, depth)
        elif task == GH_0:
            wait_weights(0, names.fore)
            for load in (loads.label, loads.scored, loads.adjp):
                load.wait()
            df = s.adjp[...].astype(F32) * s.scored[...].astype(F32)
            row = label_row()
            gh = jnp.concatenate([jnp.where(row == g, df, 0.0) for g in range(4)], axis=0)
            s.gh[...] = gh.astype(BF16)
            for block in range(2):
                row_sums(block, 7, gh)
            one.pp[512:1024, :] = nn(weights[0].fore[...], s.gh[...]).astype(BF16)
        elif task == GTF_0:
            store_with_bias(0, TF, nt(one.h[4][...], one.pp[512:1024, :]), 5)
        elif task == BACK_0:
            wait_weights(0, names.theta_b, names.back)
            end_biases(0)
            theta_b = theta(0, 0)
            one.pp[0:512, :] = theta_b
            two.h[0][0:336, :] = residual(0, theta_b).astype(BF16)
        elif task == PP_1:
            wait_weights(1, names.back, names.fore)
            loads.adjl.wait()
            gb = -(two.gb[...] * s.mask[...])
            two.gb[...] = gb
            row_sums(1, 6, gb.astype(F32))
            two.pp[0:512, :] = tn(weights[1].back[...], gb).astype(BF16)
            two.pp[512:1024, :] = nn(weights[1].fore[...], s.gh[...]).astype(BF16)
        elif task == GT_1:
            for k in range(2):
                store_with_bias(1, (TB, TF)[k], nt(two.h[4][...], two.pp[512 * k : 512 * (k + 1), :]), 4 + k)
        elif task in (DH4_1, DH4_0):
            block = int(task == DH4_1)
            if block:
                wait_weights(1, names.theta_b, names.theta_f)
            else:
                wait_weights(0, names.theta_f)
            pp, w = blocks[block].pp, weights[block]
            inward(block, 4, nn(w.theta_b[...], pp[0:512, :]) + nn(w.theta_f[...], pp[512:1024, :]))
        elif task in (B3_1, B2_1, B1_1, B3_0, B2_0, B1_0):
            block = int(task < GB_0)
            depth = 4 - (task - (B3_1 if block else B3_0))
            b, w = blocks[block], weights[block]
            dz = b.d[depth - 1][...]
            store_with_bias(block, (M0, M1, M2)[depth - 2], nt(b.h[depth - 1][...], dz), depth - 1)
            inward(block, depth - 1, nn(w[names.mid0 + depth - 2][...], dz))
        elif task in (B0_1, B0_0):
            block = int(task == B0_1)
            b = blocks[block]
            dz = b.d[0][...]
            store_with_bias(block, FIRST, nt(b.h[0][...], dz), 0)
            number, first = place_of(block, FIRST)
            rounds[number].part[first + 336 : first + 352, :] = b.bias[...].astype(BF16)
            direct = b.gb[...].astype(F32)
            din = (nn(weights[block].first[...], dz) - direct) * s.mask[...].astype(F32)
            if block:
                one.gb[...] = -(din.astype(BF16))
            else:
                s.dinput[...] = din.astype(BF16)
                hand_over(2)
        elif task == GB_0:
            gb = one.gb[...]
            row_sums(0, 6, gb.astype(F32))
            store(0, BACK, nt(gb, one.pp[0:512, :]))
            one.pp[0:512, :] = tn(weights[0].back[...], gb).astype(BF16)
        elif task == GTB_0:
            store_with_bias(0, TB, nt(one.h[4][...], one.pp[0:512, :]), 4)
        elif task == HEADS_0:
            wait_weights(0, names.theta_f)
            theta_f = theta(0, 1)
            store(0, FORE, nt(theta_f, s.gh[...]))
            s.sent[...] = heads(0, theta_f).astype(BF16)
            hand_over(0)
        elif task == THETA_1:
            wait_weights(1, names.theta_b, names.theta_f)
            end_biases(1)
            for k in range(2):
                s.tt[512 * k : 512 * (k + 1), :] = theta(1, k)
            store(1, BACK, nt(two.gb[...], s.tt[0:512, :]))
            store(1, FORE, nt(s.tt[512:1024, :], s.gh[...]))
        else:
            s.total[...] = (s.sent[...].astype(F32) + heads(1, s.tt[512:1024, :])).astype(BF16)
            hand_over(1)
            s.r2[...] = residual(1, s.tt[0:512, :]).astype(BF16)
            hand_over(3)

    def fetch(*keys):
        for block in range(2):

            @pl.when(c == block)
            def _(block=block):
                for key in keys:
                    weight_local(block, key).start()

    def send_weights(*keys):
        for block in range(2):

            @pl.when(c == block)
            def _(block=block):
                for key in keys:
                    weight_remote(block, key).start()

    barrier = pltpu.get_barrier_semaphore()
    greeted = [(other, dp, y)]
    if whole:
        greeted += [
            (c, dp1, rep1),
            (other, dp1, rep1),
            (c, dp2, rep2),
            (other, dp2, rep2),
            (c, dpz, y),
            (c, dpm, y),
        ]
    for device in greeted:
        pl.semaphore_signal(barrier, inc=1, device_id=device, device_id_type=MESH)
    loads.look.start()
    loads.past.start()
    fetch(names.first, names.hid)
    pl.semaphore_wait(barrier, len(greeted))
    send_weights(names.first, names.hid, names.mid0)
    fetch(names.mid0, names.mid1, names.mid2)
    after = {
        LOAD: ((names.fore,), (names.mid1,)),
        Z1_0: ((names.theta_b, names.back, names.backb), (names.mid2, names.fore)),
        Z2_0: ((names.theta_f, names.foreb), (names.theta_b, names.back, names.backb)),
        Z3_0: ((), (names.theta_f, names.foreb)),
    }

    sent = set()
    for item in ORDER:
        if item < STEP:
            run(item)
            if item in after:
                fetch(*after[item][0])
                send_weights(*after[item][1])
            if item == LOAD:
                for load in (loads.label, loads.scored, loads.adjp, loads.adjl):
                    load.start()
            for number in range(len(ROUNDS)):
                if not missing[number] and number not in sent:
                    sent.add(number)
                    message(number, D2D).start()
        elif whole:
            step((item - STEP) // 10, (item - STEP) % 10)
    if not whole:
        for number in range(len(ROUNDS)):
            chip_step(number)

    wait_sends()
    for key in range(11):
        for block in range(2):
            pl.when(c == block)(lambda block=block, key=key: weight_remote(block, key).wait_send())
    handed_over()
    for number, (block, _) in enumerate(ROUNDS):

        @pl.when(c == block)
        def _(number=number):
            for copy in deliver(number):
                copy.wait()


class Final(NamedTuple):
    pair: Any
    outcome: Any
    first: Any
    mid: Any
    theta: Any
    back: Any
    fore: Any
    hid: Any
    backb: Any
    foreb: Any


def widen(treedef, *refs):
    held, outs, near, wide, in_sem, out_sem = jax.tree.unflatten(treedef, refs)
    arriving = [pltpu.make_async_copy(src, dst, in_sem.at[i]) for i, (src, dst) in enumerate(zip(held, near))]
    leaving = [pltpu.make_async_copy(src, dst, out_sem.at[i]) for i, (src, dst) in enumerate(zip(wide, outs))]
    for copy in arriving:
        copy.start()
    for i, copy in enumerate(arriving):
        copy.wait()
        ref = near[i]
        if i == 2:
            wide.first[...] = ref[0:336, :].astype(F32)
            lines = ref[336:352, :].astype(F32)
            for k in range(24):
                at = k % 4 * 128
                wide.hid[k : k + 1, :] = lines[k // 4 : k // 4 + 1, at : at + 128]
            wide.backb[...] = lines[6:7, 0:336]
            wide.foreb[...] = lines[7:8, 0:256]
            for k in (7, 8, 9):
                leaving[k].start()
        else:
            wide[i][...] = ref[...].astype(F32)
        leaving[i].start()
    for copy in leaving:
        copy.wait()


def shards(whole, past, label, look, scored, adjp, adjl, first, mid, theta, back, fore, hid, backb, foreb):
    windows = past.shape[0]
    n = windows // 2
    hbm = pl.BlockSpec(memory_space=pl.ANY)
    shape = jax.ShapeDtypeStruct
    inputs = Inputs(past.T, look.T, label.reshape(windows // 128, 128), scored.T, adjp.T, adjl.T)
    given = Given(first, mid, theta, back[0].T, fore, hid.reshape(24, 128), backb, foreb)
    shapes = Results(
        (64, windows), (336, windows), (352, 512), (3, 512, 512), (2, 512, 512), (336, 512), (512, 256)
    )
    results = Results(*(shape(dims, BF16) for dims in shapes))
    buffers, structure = jax.tree.flatten(scratch(n))
    treedef = jax.tree.structure((inputs, given, results, scratch(n)))
    results = pl.pallas_call(
        functools.partial(body, n, whole, treedef),
        out_shape=results,
        in_specs=[hbm] * 14,
        out_specs=Results(*[hbm] * 7),
        scratch_shapes=buffers,
        compiler_params=pltpu.CompilerParams(
            collective_id=0, has_side_effects=True, vmem_limit_bytes=63 * 2**20
        ),
    )(*inputs, *given)

    shapes = Final(shapes.pair, shapes.outcome, (336, 512), *shapes[3:], (24, 128), (1, 336), (1, 256))
    final = Final(*(shape(dims, F32) for dims in shapes))
    near = Results(*(pltpu.VMEM(held.shape, BF16) for held in results))
    wide = Final(*(pltpu.VMEM(dims, F32) for dims in shapes))
    sems = (pltpu.SemaphoreType.DMA((7,)), pltpu.SemaphoreType.DMA((10,)))
    treedef = jax.tree.structure((results, final, near, wide, *sems))
    final = pl.pallas_call(
        functools.partial(widen, treedef),
        out_shape=final,
        in_specs=[hbm] * 7,
        out_specs=Final(*[hbm] * 10),
        scratch_shapes=[*near, *wide, *sems],
        compiler_params=pltpu.CompilerParams(vmem_limit_bytes=63 * 2**20),
    )(*results)
    if not whole:
        final = Final(*final[:2], *lax.psum(tuple(final[2:]), ("dp", "rep")))
    return (
        final.pair.T[None],
        final.outcome.T[None],
        final.first[None],
        final.mid[None],
        final.theta[None],
        final.back.T[None],
        final.fore[None],
        final.hid.reshape(1, 6, 512),
        final.backb,
        final.foreb,
    )


def solution(mesh):
    wide = P(("dp", "rep"), None)
    s2, s3, s4 = (P("section", *([None] * k)) for k in (1, 2, 3))
    in_specs = (wide, P(("dp", "rep")), wide, wide, wide, wide, s3, s4, s4, s3, s3, s3, s2, s2)
    rowwise = P("section", ("dp", "rep"), None)
    out_specs = (rowwise, rowwise, s3, s4, s4, s3, s3, s3, s2, s2)
    whole = (mesh.shape["dp"], mesh.shape["rep"]) == (8, 2)
    run = functools.partial(shards, whole)
    return jax.shard_map(run, mesh=mesh, in_specs=in_specs, out_specs=out_specs, check_vma=False)
```

time: 470 us -> 98.5 us (0.21); the launches traced: 461 us -> 97.3 us
  matrix products: 163 us -> 0 us
  waiting for transfers between devices: 129 us -> 0 us
  Pallas kernels: 0 us -> 96.5 us
  blocking collectives: 80.2 us -> 0 us
  other arithmetic: 37.4 us -> 0 us
  local copies, waits for them, and re-layouts: 21.9 us -> 0 us
  between operations: 15.3 us -> 0.84 us
  starting transfers between devices: 13.4 us -> 0 us
    dot_general x72 -> x0, matrix products: 163 us -> none  [the longest x18 37.6 us: block_forward(): jnp.dot(hidden, matrices[depth], preferred_element_type=jnp.float32)]
    psum x1 -> x0, waiting for transfers between devices: 129 us -> none  [shards(): lax.psum((cumulative_sums[0], cumulative_sums[1], cumulative_sums[2], cum...]
    pallas_call x0 -> x2, Pallas kernels: none -> 96.5 us  [the longest x1 90.9 us: shards(): pl.pallas_call(functools.partial(body, n, whole, treedef), out_shape=resu...]
    psum x1 -> x0, blocking collectives: 80.2 us -> none  [shards(): lax.psum((cumulative_sums[0], cumulative_sums[1], cumulative_sums[2], cum...]
    unnamed x209 -> x0, local copies, waits for them, and re-layouts: 20.3 us -> none
    ppermute x6 -> x0, starting transfers between devices: 13.3 us -> none  [passed_along(): return lax.ppermute(block, axis, route)]
    reduce_sum x6 -> x0, other arithmetic: 12.5 us -> none  [the longest x3 6.25 us: block_backward(): g_back_b = jnp.sum(grad_back, axis=0, dtype=jnp.float32)]
    broadcast_in_dim x4 -> x0, other arithmetic: 11.2 us -> none  [the longest x1 4.39 us: shards(): cumulative_sums[2][None]]
  transfers between devices with their start and end apart: 7 -> 0, of which waited for: 2 -> 0; matrix products, arithmetic and copies ran while one was open for 12% -> 0% of each run, Pallas kernels for 0% -> 0%
where the time goes in v1:
time: 98.5 us; the launch traced here: 97.3 us
  Pallas kernels  96.5 us (98%)
    pallas_call x1, Pallas kernels, shards(): pl.pallas_call(functools.partial(body, n, whole, treedef), out_shape=resu...  90.9 us
    pallas_call x1, Pallas kernels, shards(): pl.pallas_call(functools.partial(widen, treedef), out_shape=final, in_spe...  5.58 us

profile of v1, /device:TPU:0, one launch (start us, length us, event | category | flops | bytes accessed | tf_op | source)
XLA Modules:
  0.0 97.3 jit_solution(16373976713987128092)
XLA Ops:
  0.6 90.9 %shard_map.213 = (bf16[64,2048]{1,0:T(8,128)(2,1)}, bf16[336,2048]{1,0:T(8,128)(2,1)}, bf16[352,512]{1,0:T(8,128)(2,1)}, bf16[3,512,512]{2,1,0:T(8,128)(2,1)}, b...) custom-call(bf16[336,2048]{1,0:T(8,128)(2,1)} %bitcast.25, s32[336,2048]{1,0:T(8,128)} %bitcast.24, ...), custom_call_target="tpu_custom_call" | custom-call | tf_op jit(solution)/shard_map/pallas_call | solution.py:815
  91.6 5.6 %shard_map.214 = (f32[64,2048]{1,0:T(8,128)}, f32[336,2048]{1,0:T(8,128)}, f32[336,512]{1,0:T(8,128)}, f32[3,512,512]{2,1,0:T(8,128)}, f32[2,512,512]{2,1,0:T(8,...) custom-call(bf16[64,2048]{1,0:T(8,128)(2,1)} %get-tuple-element.27.r, ...), custom_call_target="tpu_custom_call" | custom-call | tf_op jit(solution)/shard_map/pallas_call | solution.py:832

commit v2 on v1

v2 whole, which is shorter than its diff:
```python
import functools
from typing import Any, NamedTuple

import jax
import jax.numpy as jnp
from jax import lax
from jax.experimental import pallas as pl
from jax.experimental.pallas import tpu as pltpu
from jax.sharding import PartitionSpec as P

BF16 = jnp.bfloat16
F32 = jnp.float32
MESH = pl.DeviceIdType.MESH

BACK, FORE, TB, TF, M0, M1, M2, FIRST = range(8)
PIECE_ROWS = (384, 256, 512, 512, 512, 512, 512, 384)
ROUNDS = (
    (0, (TF,)),
    (1, (TB, TF,)),
    (1, (M2, M1,)),
    (1, (M0, FIRST,)),
    (1, (BACK, FORE,)),
    (0, (BACK, FORE, TB,)),
    (0, (M2,)),
    (0, (M1,)),
    (0, (M0,)),
    (0, (FIRST,)),
)
D2D, S1, S2, S3, S4, G3, G2, G1, G1X, GD = range(10)
X, Y, Z, FAR = range(4)
ROUTES = (
    ((Z, X, Y), (X, Y, Z), 3),
    ((X, Y, Z), (Y, X, Z), 3),
    ((Y, X, Z), (Z, Y, X), 3),
    ((Z, Y, X), (Z, X, Y), 3),
    ((Y, X, Z), (X, Y, Z), 3),
    ((Y, X, Z), (Z, Y, X), 3),
    ((Z, X, Y), (X, Y, Z), 3),
    ((Z, X, Y), (X, Y, Z), 3),
    ((Y, X, Z), (X, Y, Z), 3),
    ((Y, X, Z), (X, Y, Z), 2),
)
(
    LOAD, Z1_0, Z2_0, Z3_0, Z4_0, GH_0, GTF_0, BACK_0, Z1_1, Z2_1, Z3_1, Z4_1, PP_1, GT_1, DH4_1,
    B3_1, B2_1, B1_1, B0_1, GB_0, GTB_0, DH4_0, B3_0, B2_0, B1_0, B0_0, HEADS_0, THETA_1, FINAL_1,
) = range(29)
STEP = 1000
ORDER = (
    LOAD, Z1_0, Z2_0, Z3_0, GH_0, Z4_0, BACK_0, Z1_1, Z2_1, Z3_1, PP_1, Z4_1, GT_1, DH4_1, B3_1, 1010, B2_1,
    GTF_0, B1_1, 1020, 1000, B0_1, 1011, GB_0, GTB_0, 1030, THETA_1, 1021, HEADS_0, 1001, 1040, 1012, DH4_0,
    1050, B3_0, 1022, 1002, 1031, B2_0, 1060, 1013, 1041, FINAL_1, 1070, B1_0, 1051, 1003, 1023, 1032, 1061,
    B0_0, 1042, 1080, 1014, 1071, 1090, 1052, 1033, 1004, 1062, 1043, 1081, 1072, 1015, 1024, 1091, 1053,
    1005, 1063, 1082, 1034, 1073, 1016, 1025, 1044, 1092, 1006, 1035, 1083, 1054, 1045, 1064, 1093, 1017,
    1074, 1026, 1007, 1084, 1065, 1036, 1075, 1055, 1046, 1094, 1027, 1066, 1085, 1076, 1056, 1047, 1096,
    1037, 1086, 1067, 1077, 1097, 1057, 1087,
)


def rows_of(number):
    return sum(PIECE_ROWS[piece] for piece in ROUNDS[number][1])


def place_of(block, piece):
    for number, (at, pieces) in enumerate(ROUNDS):
        if at == block and piece in pieces:
            return number, sum(PIECE_ROWS[p] for p in pieces[: pieces.index(piece)])


def rounds_of(block):
    return [number for number, (at, _) in enumerate(ROUNDS) if at == block]


def parts_of(block):
    parts = []
    for number, (at, pieces) in enumerate(ROUNDS):
        first = 0
        half = rows_of(number) // 2
        for piece in pieces if at == block else ():
            count = (336, 256, 512, 512, 512, 512, 512, 352)[piece]
            for core in range(2):
                low, high = max(first, core * half), min(first + count, (core + 1) * half)
                if low < high:
                    parts += [(number, core, low - core * half, high - low, piece, low - first)] * (1 + (piece == FORE))
            first += PIECE_ROWS[piece]
    return parts


def nn(a, b):
    return jnp.dot(a, b, preferred_element_type=F32)


def nt(a, b):
    return lax.dot_general(a, b, (((1,), (1,)), ((), ())), preferred_element_type=F32)


def tn(a, b):
    return lax.dot_general(a, b, (((0,), (0,)), ((), ())), preferred_element_type=F32)


class Inputs(NamedTuple):
    past: Any
    look: Any
    label: Any
    scored: Any
    adjp: Any
    adjl: Any


class Given(NamedTuple):
    first: Any
    mid: Any
    theta: Any
    back: Any
    fore: Any
    hid: Any
    backb: Any
    foreb: Any


class Gathered(NamedTuple):
    own: Any
    rest: Any


class Results(NamedTuple):
    pair: Any
    outcome: Any
    rounds: Any


class Weights(NamedTuple):
    first: Any
    hid: Any
    mid0: Any
    mid1: Any
    mid2: Any
    theta: Any
    back: Any
    backb: Any
    fore: Any
    foreb: Any


class Block(NamedTuple):
    h: Any
    d: Any
    gb: Any
    pp: Any
    bias: Any
    hid: Any
    backb: Any
    foreb: Any


class Round(NamedTuple):
    part: Any
    landing: Any


class Scratch(NamedTuple):
    weights: Any
    blocks: Any
    rounds: Any
    observed: Any
    mask: Any
    label: Any
    scored: Any
    adjp: Any
    gh: Any
    tt: Any
    sent: Any
    total: Any
    dinput: Any
    r2: Any
    load_sem: Any
    weight_sem: Any
    weight_send: Any
    send_sem: Any
    recv_sem: Any
    last_send: Any
    last_recv: Any
    give_send: Any
    give_recv: Any


def scratch(n):
    def weights():
        square = pltpu.VMEM((512, 512), BF16)
        return Weights(
            first=pltpu.VMEM((336, 512), BF16),
            hid=pltpu.VMEM((24, 128), F32),
            mid0=square,
            mid1=square,
            mid2=square,
            theta=pltpu.VMEM((2, 512, 512), BF16),
            back=pltpu.VMEM((336, 512), BF16),
            backb=pltpu.VMEM((1, 336), F32),
            fore=pltpu.VMEM((512, 256), BF16),
            foreb=pltpu.VMEM((1, 256), F32),
        )

    def block():
        return Block(
            h=[pltpu.VMEM(((336 if k == 0 else 512) + 16, n), BF16) for k in range(5)],
            d=[pltpu.VMEM((512, n), BF16) for _ in range(4)],
            gb=pltpu.VMEM((336, n), BF16),
            pp=pltpu.VMEM((1024, n), BF16),
            bias=pltpu.VMEM((16, 512), F32),
            hid=pltpu.VMEM((512, 8), F32),
            backb=pltpu.VMEM((336, 8), F32),
            foreb=pltpu.VMEM((256, 8), F32),
        )

    def a_round(number):
        rows = rows_of(number)
        half = rows // 2

        shapes = [(half, 512)]
        for _ in range(ROUTES[number][2]):
            tall, wide = shapes[-1]
            shapes.append((tall // 2, wide) if tall // 2 % 16 == 0 else (tall, wide // 2))
        shapes += [shapes[-1]] * (5 - len(shapes))
        return Round(
            part=pltpu.VMEM((rows, 512), BF16),
            landing=[pltpu.VMEM(shape, BF16) for shape in shapes[1:]],
        )

    dma = pltpu.SemaphoreType.DMA
    count = len(ROUNDS)
    most = max(len(rounds_of(0)), len(rounds_of(1)))
    return Scratch(
        weights=[weights(), weights()],
        blocks=[block(), block()],
        rounds=[a_round(number) for number in range(count)],
        observed=pltpu.VMEM((336, n), jnp.int32),
        mask=pltpu.VMEM((336, n), BF16),
        label=pltpu.VMEM((n // 128, 128), jnp.int32),
        scored=pltpu.VMEM((64, n), jnp.int32),
        adjp=pltpu.VMEM((64, n), BF16),
        gh=pltpu.VMEM((256, n), BF16),
        tt=pltpu.VMEM((1024, n), BF16),
        sent=pltpu.VMEM((64, n), BF16),
        total=pltpu.VMEM((64, n), BF16),
        dinput=pltpu.VMEM((336, n), BF16),
        r2=pltpu.VMEM((336, n), BF16),
        load_sem=dma((6,)),
        weight_sem=dma((2, 10)),
        weight_send=dma((10,)),
        send_sem=dma((count,)),
        recv_sem=dma((count, 5)),
        last_send=dma((most,)),
        last_recv=dma((most, 2)),
        give_send=dma((4,)),
        give_recv=dma((4,)),
    )


def body(n, whole, treedef, *refs):
    inputs, given, outs, s = jax.tree.unflatten(treedef, refs)
    weights, blocks = s.weights, s.blocks
    rounds = [Round(r.part, [place.own, *r.landing]) for r, place in zip(s.rounds, outs.rounds)]

    c = lax.axis_index("section")
    dp = lax.axis_index("dp")
    y = lax.axis_index("rep")
    z = lax.div(dp, 2)
    x = lax.rem(dp, 2)
    other = 1 - c
    dpx = dp + 1 - 2 * x
    dpz = dp + 2 - 4 * lax.rem(z, 2)
    dpm = 2 * (3 - z) + x
    ry = 1 - y
    chips = ((dpx, y), (dp, ry), (dpz, y), (dpm, y))
    sides = (x, y, lax.rem(lax.div(z + 1, 2), 2))

    def by_core(pair):
        return pair[0] if pair[0] is pair[1] else jnp.where(c == 0, *pair)

    def chip(number, stage):
        if stage == 3:
            return chips[FAR]
        axes = [ROUTES[number][core][stage] for core in range(2)]
        return tuple(by_core([chips[axis][i] for axis in axes]) for i in range(2))

    def side(number, stage, flip=False):
        axes = [ROUTES[number][core ^ flip][stage] for core in range(2)]
        return by_core([sides[axis] for axis in axes])

    mine = pl.ds(pl.multiple_of(c * n, 128), n)
    label_rows = n // 128
    loads = Inputs(
        past=(inputs.past.at[:, mine], blocks[0].h[0].at[pl.ds(0, 336)]),
        look=(inputs.look.at[:, mine], s.observed),
        label=(inputs.label.at[pl.ds(pl.multiple_of(c * label_rows, 8), label_rows)], s.label),
        scored=(inputs.scored.at[:, mine], s.scored),
        adjp=(inputs.adjp.at[:, mine], s.adjp),
        adjl=(inputs.adjl.at[:, mine], blocks[1].gb),
    )
    loads = Inputs(*(pltpu.make_async_copy(*pair, s.load_sem.at[i]) for i, pair in enumerate(loads)))
    sources = Weights(
        first=given.first.at[0],
        hid=given.hid,
        mid0=given.mid.at[0, 0],
        mid1=given.mid.at[0, 1],
        mid2=given.mid.at[0, 2],
        theta=given.theta.at[0],
        back=given.back,
        backb=given.backb,
        fore=given.fore.at[0],
        foreb=given.foreb,
    )

    def weight_local(block, i):
        return pltpu.make_async_copy(sources[i], weights[block][i], s.weight_sem.at[block, i])

    def weight_remote(block, i):
        return pltpu.make_async_remote_copy(
            sources[i],
            weights[block][i],
            s.weight_send.at[i],
            s.weight_sem.at[block, i],
            device_id=(other, dp, y),
            device_id_type=MESH,
        )

    names = Weights(*range(10))

    waited = set()

    def wait_weights(block, *keys):
        for key in keys:
            if (block, key) not in waited:
                waited.add((block, key))
                weight_local(block, key).wait()

    def regions(number, base):
        keep, give = [(base, rows_of(number) // 2, 0, 512)], [None]
        for stage in range(ROUTES[number][2]):
            row, rows, col, cols = keep[-1]
            bit = side(number, stage)
            if rows // 2 % 16 == 0:
                rows = rows // 2
                keep.append((row + bit * rows, rows, col, cols))
                give.append((row + (1 - bit) * rows, rows, col, cols))
            else:
                cols = cols // 2
                keep.append((row, rows, col + bit * cols, cols))
                give.append((row, rows, col + (1 - bit) * cols, cols))

        def at(row, rows, col, cols):
            across = slice(None) if cols == 512 else pl.ds(pl.multiple_of(col, 128), cols)
            return (pl.ds(pl.multiple_of(row, 16), rows), across)

        return [at(*area) for area in keep], [area and at(*area) for area in give]

    def summed(number):
        return regions(number, c * (rows_of(number) // 2))

    def message(number, kind):
        r = rounds[number]
        halvings = ROUTES[number][2]
        half = rows_of(number) // 2
        if kind == D2D:
            where = (pl.ds(pl.multiple_of(other * half, 16), half), slice(None))
            src, dst, device = r.part.at[where], r.landing[D2D], (other, dp, y)
        elif kind <= S4:
            keep, give = summed(number)
            src, dst = r.part.at[give[kind] if kind <= halvings else keep[-1]], r.landing[kind]
            device = (c, *chip(number, kind - S1))
        else:
            stage = {G3: 2, G2: 1, G1: 0, G1X: 0, GD: 0}[kind]
            where = regions(number, 0)[0][stage + 1 if whole else 0]
            src = r.landing[D2D].at[where]
            dst = src if kind <= G1 else outs.rounds[number].rest.at[where]
            device = (other, dp, y) if kind == GD else (other if kind == G1X else c, *chip(number, stage))
        return pltpu.make_async_remote_copy(
            src, dst, *semaphores(number, kind), device_id=device, device_id_type=MESH
        )

    def semaphores(number, kind):
        place = rounds_of(ROUNDS[number][0]).index(number)
        send = s.last_send.at[place] if kind == GD else s.send_sem.at[number]
        if kind >= G1X:
            return send, s.last_recv.at[place, kind - G1X]
        return send, s.recv_sem.at[number, {G1: D2D, G2: S1, G3: S2}.get(kind, kind)]

    latest = {}

    def begin(number, kind):
        if number in latest:
            message(number, latest[number]).wait_send()
        latest[number] = kind
        message(number, kind).start()

    def fold(number, kind, where, *buffer):
        part = rounds[number].part
        part[where] = part[where] + rounds[number].landing[kind][buffer]

    def fold_and_send(number, kind):
        keep, give = summed(number)
        level = kind + 1
        bit = side(number, kind)
        rows, cols = rounds[number].landing[kind].shape

        def of_landing(bit):
            if rows // 2 % 16 == 0:
                return (pl.ds(pl.multiple_of(bit * (rows // 2), 16), rows // 2), slice(None))
            return (slice(None), pl.ds(pl.multiple_of(bit * (cols // 2), 128), cols // 2))

        fold(number, kind, give[level], *of_landing(1 - bit))
        begin(number, level)
        fold(number, kind, keep[level], *of_landing(bit))

    def settle(number, kind):
        r = rounds[number]
        here = regions(number, 0)[0][-1]
        r.landing[D2D][here] = r.part[summed(number)[0][-1]] + r.landing[kind][...]

    def chip_step(number):
        block = ROUNDS[number][0]
        message(number, D2D).wait_recv()
        settle_half(number)
        finish(number)

        pl.when(c == block)(lambda: message(number, GD).wait_recv())

    def settle_half(number):
        r = rounds[number]
        r.landing[D2D][...] = r.landing[D2D][...] + r.part[summed(number)[0][0]]

    def finish(number):
        block = ROUNDS[number][0]
        message(number, latest.pop(number)).wait_send()
        if whole:
            pl.when(c == block)(lambda: message(number, G1).start())
            pl.when(c != block)(lambda: message(number, G1X).start())
        pl.when(c != block)(lambda: message(number, GD).start())

    def step(number, kind):
        block = ROUNDS[number][0]
        halvings = ROUTES[number][2]
        if kind < G1:
            message(number, kind).wait_recv()
        if kind < halvings:
            fold_and_send(number, kind)
        elif kind < S4:
            if kind > halvings:
                message(number, latest.pop(number)).wait_send()
            fold(number, kind, summed(number)[0][-1], ...)
            begin(number, kind + 1)
        elif kind < G1:
            if kind == S4:
                settle(number, kind)
            following = G1 + 1 - halvings if kind == S4 else kind + 1
            if following < G1:
                begin(number, following)
            else:
                finish(number)
        else:

            @pl.when(c == block)
            def _():
                quarter = rows_of(number) // 4
                theirs = side(number, 0, flip=True)
                for kind, ref, at in (
                    (G1, rounds[number].landing[D2D], 1 - side(number, 0)),
                    (GD, outs.rounds[number].rest, theirs),
                    (G1X, outs.rounds[number].rest, 1 - theirs),
                ):
                    ref = ref.at[pl.ds(pl.multiple_of(at * quarter, 16), quarter)]
                    pltpu.make_async_remote_copy(
                        ref, ref, *semaphores(number, kind), device_id=(other, dp, y), device_id_type=MESH
                    ).wait_recv()

    def wait_sends():
        for number, (block, _) in enumerate(ROUNDS):
            if whole:
                pl.when(c == block)(lambda number=number: message(number, G1).wait_send())
                pl.when(c != block)(lambda number=number: message(number, G1X).wait_send())
            pl.when(c != block)(lambda number=number: message(number, GD).wait_send())

    def result(i):
        src = (s.sent, s.total, s.dinput, s.r2)[i]
        dst = (outs.pair, outs.outcome)[i // 2].at[:, mine]
        local = pltpu.make_async_copy(src, dst, s.give_send.at[i])
        remote = pltpu.make_async_remote_copy(
            src, dst, s.give_send.at[i], s.give_recv.at[i], device_id=(other, dp, y), device_id_type=MESH
        )
        return i % 2, local, remote

    def hand_over(i):
        keeper, local, remote = result(i)
        pl.when(c == keeper)(lambda: local.start())
        pl.when(c != keeper)(lambda: remote.start())

    def handed_over():
        for i in range(4):
            keeper, local, remote = result(i)

            @pl.when(c == keeper)
            def _(local=local, remote=remote):
                local.wait()
                remote.wait_recv()

            pl.when(c != keeper)(lambda remote=remote: remote.wait_send())

    missing = [set(pieces) for _, pieces in ROUNDS]

    def store(block, piece, value):
        number, first = place_of(block, piece)
        missing[number].discard(piece)
        value = value.astype(BF16)
        part = rounds[number].part
        if piece == FORE:
            for k in range(2):
                part[first : first + 256, 256 * k : 256 * (k + 1)] = value[256 * k : 256 * (k + 1)]
        else:
            part[first : first + value.shape[0], :] = value

    def store_with_bias(block, piece, value, row):
        k = value.shape[0] - 16
        blocks[block].bias[row : row + 1, :] = value[k : k + 1]
        store(block, piece, value[:k])

    def row_sums(block, row, value):
        folded = value[:, 0:128]
        for i in range(1, n // 128):
            folded = folded + value[:, 128 * i : 128 * (i + 1)]
        sums = nt(jnp.ones((16, 128), BF16), folded.astype(BF16))
        blocks[block].bias[row : row + 1, 0 : value.shape[0]] = sums[0:1]

    def layer(block, depth):
        b, w = blocks[block], weights[block]
        h = b.h[depth - 1]
        zed = tn(w[(names.first, names.mid0, names.mid1, names.mid2)[depth - 1]][...], h[0 : h.shape[0] - 16, :])
        zed = zed + b.hid[:, depth - 1 : depth]
        sig = 0.5 * jnp.tanh(0.5 * zed) + 0.5
        out = zed * sig
        b.h[depth][0:512, :] = out.astype(BF16)
        b.d[depth - 1][...] = (sig + out * (1.0 - sig)).astype(BF16)

    def theta(block, k):
        return (tn(weights[block].theta[k], blocks[block].h[4][0:512, :]) + blocks[block].hid[:, 4 + k : 5 + k]).astype(BF16)

    def heads(block, theta_f):
        wide = tn(weights[block].fore[...], theta_f) + blocks[block].foreb[:, 0:1]
        row = label_row()
        chosen = jnp.zeros((64, n), F32)
        for g in range(4):
            chosen = chosen + jnp.where(row == g, wide[64 * g : 64 * (g + 1)], 0.0)
        return chosen * s.scored[...].astype(F32)

    def residual(block, theta_b):
        backcast = nn(weights[block].back[...], theta_b) + blocks[block].backb[:, 0:1]
        return (blocks[block].h[0][0:336, :].astype(F32) - backcast) * s.mask[...].astype(F32)

    def inward(block, depth, dh):
        d = blocks[block].d[depth - 1]
        d[...] = (dh * d[...].astype(F32)).astype(BF16)

    def layer_biases(block):
        b, w = blocks[block], weights[block]
        lines = [
            jnp.concatenate([w.hid[4 * k + i : 4 * k + i + 1, :] for i in range(4)], axis=1) for k in range(6)
        ]
        lines.append(jnp.zeros((2, 512), F32))
        b.hid[...] = jnp.concatenate(lines, axis=0).T

    def end_biases(block):
        b, w = blocks[block], weights[block]
        b.backb[...] = jnp.broadcast_to(w.backb[...], (8, 336)).T
        b.foreb[...] = jnp.broadcast_to(w.foreb[...], (8, 256)).T

    def label_row():
        return jnp.concatenate([s.label[i : i + 1, :] for i in range(label_rows)], axis=1)

    def run(task):
        one, two = blocks
        if task == LOAD:
            loads.look.wait()
            mask = s.observed[...].astype(F32).astype(BF16)
            s.mask[...] = mask
            loads.past.wait()
            one.h[0][0:336, :] = one.h[0][0:336, :] * mask
            wait_weights(0, names.hid)
            layer_biases(0)
        elif task in (Z1_0, Z2_0, Z3_0, Z4_0):
            depth = task - Z1_0 + 1
            if depth == 1:
                wait_weights(0, names.first, names.mid0)
            elif depth == 3:
                wait_weights(0, names.mid1, names.mid2)
            layer(0, depth)
        elif task in (Z1_1, Z2_1, Z3_1, Z4_1):
            depth = task - Z1_1 + 1
            if depth == 1:
                wait_weights(1, *range(10))
                layer_biases(1)
            layer(1, depth)
        elif task == GH_0:
            wait_weights(0, *late)
            for load in (loads.label, loads.scored, loads.adjp, loads.adjl):
                load.wait()
            for b in blocks:
                for h in b.h:
                    k = h.shape[0] - 16
                    h[k : k + 16, :] = jnp.ones((16, n), BF16)
                b.bias[...] = jnp.zeros((16, 512), F32)
            df = s.adjp[...].astype(F32) * s.scored[...].astype(F32)
            row = label_row()
            gh = jnp.concatenate([jnp.where(row == g, df, 0.0) for g in range(4)], axis=0)
            s.gh[...] = gh.astype(BF16)
            for block in range(2):
                row_sums(block, 7, gh)
            one.pp[512:1024, :] = nn(weights[0].fore[...], s.gh[...]).astype(BF16)
        elif task == GTF_0:
            store_with_bias(0, TF, nt(one.h[4][...], one.pp[512:1024, :]), 5)
        elif task == BACK_0:
            end_biases(0)
            theta_b = theta(0, 0)
            one.pp[0:512, :] = theta_b
            two.h[0][0:336, :] = residual(0, theta_b).astype(BF16)
        elif task == PP_1:
            gb = -(two.gb[...] * s.mask[...])
            two.gb[...] = gb
            row_sums(1, 6, gb.astype(F32))
            two.pp[0:512, :] = tn(weights[1].back[...], gb).astype(BF16)
            two.pp[512:1024, :] = nn(weights[1].fore[...], s.gh[...]).astype(BF16)
        elif task == GT_1:
            for k in range(2):
                store_with_bias(1, (TB, TF)[k], nt(two.h[4][...], two.pp[512 * k : 512 * (k + 1), :]), 4 + k)
        elif task in (DH4_1, DH4_0):
            block = int(task == DH4_1)
            pp, w = blocks[block].pp, weights[block]
            inward(block, 4, nn(w.theta[0], pp[0:512, :]) + nn(w.theta[1], pp[512:1024, :]))
        elif task in (B3_1, B2_1, B1_1, B3_0, B2_0, B1_0):
            block = int(task < GB_0)
            depth = 4 - (task - (B3_1 if block else B3_0))
            b, w = blocks[block], weights[block]
            dz = b.d[depth - 1][...]
            store_with_bias(block, (M0, M1, M2)[depth - 2], nt(b.h[depth - 1][...], dz), depth - 1)
            inward(block, depth - 1, nn(w[names.mid0 + depth - 2][...], dz))
        elif task in (B0_1, B0_0):
            block = int(task == B0_1)
            b = blocks[block]
            dz = b.d[0][...]
            store_with_bias(block, FIRST, nt(b.h[0][...], dz), 0)
            number, first = place_of(block, FIRST)
            rounds[number].part[first + 336 : first + 352, :] = b.bias[...].astype(BF16)
            direct = b.gb[...].astype(F32)
            din = (nn(weights[block].first[...], dz) - direct) * s.mask[...].astype(F32)
            if block:
                one.gb[...] = -(din.astype(BF16))
            else:
                s.dinput[...] = din.astype(BF16)
                hand_over(2)
        elif task == GB_0:
            gb = one.gb[...]
            row_sums(0, 6, gb.astype(F32))
            store(0, BACK, nt(gb, one.pp[0:512, :]))
            one.pp[0:512, :] = tn(weights[0].back[...], gb).astype(BF16)
        elif task == GTB_0:
            store_with_bias(0, TB, nt(one.h[4][...], one.pp[0:512, :]), 4)
        elif task == HEADS_0:
            theta_f = theta(0, 1)
            store(0, FORE, nt(theta_f, s.gh[...]))
            s.sent[...] = heads(0, theta_f).astype(BF16)
            hand_over(0)
        elif task == THETA_1:
            end_biases(1)
            for k in range(2):
                s.tt[512 * k : 512 * (k + 1), :] = theta(1, k)
            store(1, BACK, nt(two.gb[...], s.tt[0:512, :]))
            store(1, FORE, nt(s.tt[512:1024, :], s.gh[...]))
        else:
            s.total[...] = (s.sent[...].astype(F32) + heads(1, s.tt[512:1024, :])).astype(BF16)
            hand_over(1)
            s.r2[...] = residual(1, s.tt[0:512, :]).astype(BF16)
            hand_over(3)

    def fetch(*keys):
        for block in range(2):

            @pl.when(c == block)
            def _(block=block):
                for key in keys:
                    weight_local(block, key).start()

    def send_weights(*keys):
        for block in range(2):

            @pl.when(c == block)
            def _(block=block):
                for key in keys:
                    weight_remote(block, key).start()

    barrier = pltpu.get_barrier_semaphore()
    greeted = [(other, dp, y)]
    if whole:
        greeted += [(c, *place) for place in chips] + [(other, *place) for place in chips[:FAR]]
    for device in greeted:
        pl.semaphore_signal(barrier, inc=1, device_id=device, device_id_type=MESH)
    loads.look.start()
    loads.past.start()
    fetch(names.first, names.hid, names.mid0)
    pl.semaphore_wait(barrier, len(greeted))
    send_weights(names.first, names.hid, names.mid0)
    late = (names.fore, names.theta, names.back, names.backb, names.foreb)
    after = {LOAD: ((names.mid1, names.mid2, *late), (names.mid1, names.mid2)), Z2_0: ((), late)}

    sent = set()
    for item in ORDER:
        if item < STEP:
            run(item)
            if item in after:
                fetch(*after[item][0])
                send_weights(*after[item][1])
            if item == LOAD:
                for load in (loads.label, loads.scored, loads.adjp, loads.adjl):
                    load.start()
            for number in range(len(ROUNDS)):
                if not missing[number] and number not in sent:
                    sent.add(number)
                    begin(number, D2D)
        elif whole:
            step((item - STEP) // 10, (item - STEP) % 10)
    if not whole:
        for number in range(len(ROUNDS)):
            chip_step(number)

    wait_sends()
    for key in range(10):
        for block in range(2):
            pl.when(c == block)(lambda block=block, key=key: weight_remote(block, key).wait_send())
    handed_over()


class Final(NamedTuple):
    pair: Any
    outcome: Any
    first: Any
    mid: Any
    theta: Any
    back: Any
    fore: Any
    hid: Any
    backb: Any
    foreb: Any


def widen(treedef, *refs):
    held, outs, wide, sem = jax.tree.unflatten(treedef, refs)
    names = Final(*range(10))

    def leaving(i):
        return pltpu.make_async_copy(wide[i], outs[i], sem.at[i])

    def take(block):
        parts = parts_of(block)
        for i, part in enumerate(parts):
            number, core, low, count, piece, first = part
            source = held.rounds[number].own if core == block else held.rounds[number].rest
            rows = source[low : low + count, :].astype(F32)
            if piece == FORE:
                k = int(parts[i - 1] == part)
                wide.fore[256 * k + first : 256 * k + first + count, :] = rows[:, 256 * k : 256 * (k + 1)]
            elif piece == FIRST:
                used = min(count, 336 - first)
                wide.first[first : first + used, :] = rows[:used]
                if used < count:
                    lines = rows[used : used + 8]
                    for k in range(24):
                        at = k % 4 * 128
                        wide.hid[k : k + 1, :] = lines[k // 4 : k // 4 + 1, at : at + 128]
                    wide.backb[...] = lines[6:7, 0:336]
                    wide.foreb[...] = lines[7:8, 0:256]
            elif piece == BACK:
                wide.back[first : first + count, :] = rows
            elif piece in (TB, TF):
                wide.theta[piece - TB, first : first + count, :] = rows
            else:
                wide.mid[piece - M0, first : first + count, :] = rows

    wide.outcome[...] = held.outcome[...].astype(F32)
    leaving(names.outcome).start()
    wide.pair[...] = held.pair[...].astype(F32)
    leaving(names.pair).start()
    c = lax.axis_index("section")
    for block in range(2):
        pl.when(c == block)(functools.partial(take, block))
    for i in range(2, 10):
        leaving(i).start()
    for i in range(10):
        leaving(i).wait()


def shards(whole, past, label, look, scored, adjp, adjl, first, mid, theta, back, fore, hid, backb, foreb):
    windows = past.shape[0]
    n = windows // 2
    hbm = pl.BlockSpec(memory_space=pl.ANY)
    shape = jax.ShapeDtypeStruct
    inputs = Inputs(past.T, look.T, label.reshape(windows // 128, 128), scored.T, adjp.T, adjl.T)
    given = Given(first, mid, theta, back[0].T, fore, hid.reshape(24, 128), backb, foreb)
    results = Results(
        pair=pltpu.VMEM((64, windows), BF16),
        outcome=pltpu.VMEM((336, windows), BF16),
        rounds=[
            Gathered(*[pltpu.VMEM((rows_of(number) // 2, 512), BF16)] * 2) for number in range(len(ROUNDS))
        ],
    )
    buffers = jax.tree.leaves(scratch(n))
    treedef = jax.tree.structure((inputs, given, results, scratch(n)))
    near = pl.BlockSpec(memory_space=pltpu.VMEM)
    places = jax.tree.leaves(results)
    held = pl.pallas_call(
        functools.partial(body, n, whole, treedef),
        out_shape=places,
        in_specs=[hbm] * 14,
        out_specs=[near] * len(places),
        scratch_shapes=buffers,
        compiler_params=pltpu.CompilerParams(
            collective_id=0, has_side_effects=True, vmem_limit_bytes=54 * 2**20
        ),
    )(*inputs, *given)

    shapes = Final(
        pair=(64, windows),
        outcome=(336, windows),
        first=(336, 512),
        mid=(3, 512, 512),
        theta=(2, 512, 512),
        back=(336, 512),
        fore=(512, 256),
        hid=(24, 128),
        backb=(1, 336),
        foreb=(1, 256),
    )
    final = Final(*(shape(dims, F32) for dims in shapes))
    wide = Final(*(pltpu.VMEM(dims, F32) for dims in shapes))
    sem = pltpu.SemaphoreType.DMA((10,))
    treedef = jax.tree.structure((results, final, wide, sem))
    final = pl.pallas_call(
        functools.partial(widen, treedef),
        out_shape=final,
        in_specs=[near] * len(places),
        out_specs=Final(*[hbm] * 10),
        scratch_shapes=[*wide, sem],
        compiler_params=pltpu.CompilerParams(vmem_limit_bytes=32 * 2**20),
    )(*held)
    if not whole:
        final = Final(*final[:2], *lax.psum(tuple(final[2:]), ("dp", "rep")))
    return (
        final.pair.T[None],
        final.outcome.T[None],
        final.first[None],
        final.mid[None],
        final.theta[None],
        final.back.T[None],
        final.fore[None],
        final.hid.reshape(1, 6, 512),
        final.backb,
        final.foreb,
    )


def solution(mesh):
    wide = P(("dp", "rep"), None)
    s2, s3, s4 = (P("section", *([None] * k)) for k in (1, 2, 3))
    in_specs = (wide, P(("dp", "rep")), wide, wide, wide, wide, s3, s4, s4, s3, s3, s3, s2, s2)
    rowwise = P("section", ("dp", "rep"), None)
    out_specs = (rowwise, rowwise, s3, s4, s4, s3, s3, s3, s2, s2)
    whole = (mesh.shape["dp"], mesh.shape["rep"]) == (8, 2)
    run = functools.partial(shards, whole)
    return jax.shard_map(run, mesh=mesh, in_specs=in_specs, out_specs=out_specs, check_vma=False)
```

time: 98.5 us -> 87.5 us (0.89)
  Pallas kernels: 96.5 us -> 86.5 us
    pallas_call x1, Pallas kernels: 90.9 us -> 82.2 us  [shards(): pl.pallas_call(functools.partial(body, n, whole, treedef), out_shape=plac...]
    pallas_call x1, Pallas kernels: 5.58 us -> 4.26 us  [shards(): pl.pallas_call(functools.partial(widen, treedef), out_shape=final, in_spe...]
where the time goes in v2:
time: 87.5 us; the launch traced here: 87.3 us
  Pallas kernels  86.5 us (99%)
    pallas_call x1, Pallas kernels, shards(): pl.pallas_call(functools.partial(body, n, whole, treedef), out_shape=plac...  82.2 us
    pallas_call x1, Pallas kernels, shards(): pl.pallas_call(functools.partial(widen, treedef), out_shape=final, in_spe...  4.26 us

profile of v2, /device:TPU:0, one launch (start us, length us, event | category | flops | bytes accessed | tf_op | source)
XLA Modules:
  0.0 87.3 jit_solution(3518079254380475514)
XLA Ops:
  0.6 82.2 %shard_map.213 = (bf16[64,2048]{1,0:T(8,128)(2,1)S(1)}, bf16[336,2048]{1,0:T(8,128)(2,1)S(1)}, bf16[256,512]{1,0:T(8,128)(2,1)S(1)}, bf16[256,512]{1,0:T(8,128)(...) custom-call(bf16[336,2048]{1,0:T(8,128)(2,1)} %bitcast.25, ...), custom_call_target="tpu_custom_call" | custom-call | tf_op jit(solution)/shard_map/pallas_call | solution.py:815
  82.8 4.3 %shard_map.214 = (f32[64,2048]{1,0:T(8,128)}, f32[336,2048]{1,0:T(8,128)}, f32[336,512]{1,0:T(8,128)}, f32[3,512,512]{2,1,0:T(8,128)}, f32[2,512,512]{2,1,0:T(8,...) custom-call(bf16[64,2048]{1,0:T(8,128)(2,1)S(1)} %get-tuple-element., ...), custom_call_target="tpu_custom_call" | custom-call | tf_op jit(solution)/shard_map/pallas_call | solution.py:842

commit v3 on v2

--- a/solution.py
+++ b/solution.py
@@ -17,7 +17,8 @@
 ROUNDS = (
     (0, (TF,)),
     (1, (TB, TF,)),
-    (1, (M2, M1,)),
+    (1, (M2,)),
+    (1, (M1,)),
     (1, (M0, FIRST,)),
     (1, (BACK, FORE,)),
     (0, (BACK, FORE, TB,)),
@@ -29,30 +30,31 @@
 D2D, S1, S2, S3, S4, G3, G2, G1, G1X, GD = range(10)
 X, Y, Z, FAR = range(4)
 ROUTES = (
-    ((Z, X, Y), (X, Y, Z), 3),
-    ((X, Y, Z), (Y, X, Z), 3),
-    ((Y, X, Z), (Z, Y, X), 3),
-    ((Z, Y, X), (Z, X, Y), 3),
-    ((Y, X, Z), (X, Y, Z), 3),
-    ((Y, X, Z), (Z, Y, X), 3),
-    ((Z, X, Y), (X, Y, Z), 3),
-    ((Z, X, Y), (X, Y, Z), 3),
-    ((Y, X, Z), (X, Y, Z), 3),
-    ((Y, X, Z), (X, Y, Z), 2),
+    ((X, Z, Y), (Y, X, Z)),
+    ((Y, Z, X), (X, Y, Z)),
+    ((Y, X, Z), (Y, X, Z)),
+    ((X, Z, Y), (Z, Y, X)),
+    ((Z, X, Y), (X, Y, Z)),
+    ((Z, Y, X), (X, Y, Z)),
+    ((Y, X, Z), (Z, Y, X)),
+    ((Y, X, Z), (X, Z, Y)),
+    ((Z, Y, X), (X, Y, Z)),
+    ((X, Y, Z), (Y, X, Z)),
+    ((Y, X, Z), (X, Y, Z)),
 )
 (
     LOAD, Z1_0, Z2_0, Z3_0, Z4_0, GH_0, GTF_0, BACK_0, Z1_1, Z2_1, Z3_1, Z4_1, PP_1, GT_1, DH4_1,
-    B3_1, B2_1, B1_1, B0_1, GB_0, GTB_0, DH4_0, B3_0, B2_0, B1_0, B0_0, HEADS_0, THETA_1, FINAL_1,
-) = range(29)
+    B3_1, B2_1, B1_1, B0_1, GB_0, GTB_0, DH4_0, B3_0, B2_0, B1_0, B0_0, HEADS_0, THETA_1, FINAL_1, GTF_1,
+) = range(30)
 STEP = 1000
 ORDER = (
-    LOAD, Z1_0, Z2_0, Z3_0, GH_0, Z4_0, BACK_0, Z1_1, Z2_1, Z3_1, PP_1, Z4_1, GT_1, DH4_1, B3_1, 1010, B2_1,
-    GTF_0, B1_1, 1020, 1000, B0_1, 1011, GB_0, GTB_0, 1030, THETA_1, 1021, HEADS_0, 1001, 1040, 1012, DH4_0,
-    1050, B3_0, 1022, 1002, 1031, B2_0, 1060, 1013, 1041, FINAL_1, 1070, B1_0, 1051, 1003, 1023, 1032, 1061,
-    B0_0, 1042, 1080, 1014, 1071, 1090, 1052, 1033, 1004, 1062, 1043, 1081, 1072, 1015, 1024, 1091, 1053,
-    1005, 1063, 1082, 1034, 1073, 1016, 1025, 1044, 1092, 1006, 1035, 1083, 1054, 1045, 1064, 1093, 1017,
-    1074, 1026, 1007, 1084, 1065, 1036, 1075, 1055, 1046, 1094, 1027, 1066, 1085, 1076, 1056, 1047, 1096,
-    1037, 1086, 1067, 1077, 1097, 1057, 1087,
+    LOAD, Z1_0, Z2_0, Z3_0, Z4_0, BACK_0, Z1_1, GH_0, Z2_1, PP_1, Z3_1, Z4_1, GT_1, GTF_1, DH4_1, B3_1, 1010,
+    B2_1, B1_1, B0_1, 1020, 1030, GB_0, 1011, 1040, HEADS_0, GTF_0, GTB_0, 1031, DH4_0, 1000, 1021, 1060,
+    1012, THETA_1, 1041, B3_0, 1001, 1050, 1032, 1022, B2_0, 1070, 1061, 1013, B1_0, 1080, 1002, 1042, 1033,
+    1051, FINAL_1, 1071, 1023, 1090, B0_0, 1062, 1014, 1081, 1003, 1100, 1052, 1043, 1024, 1091, 1072, 1034,
+    1015, 1063, 1082, 1053, 1101, 1004, 1092, 1025, 1073, 1035, 1044, 1016, 1102, 1083, 1005, 1026, 1064,
+    1093, 1054, 1036, 1045, 1103, 1074, 1006, 1084, 1065, 1094, 1055, 1104, 1046, 1075, 1085, 1095, 1066,
+    1105, 1056, 1086, 1076, 1096, 1106,
 )
 
 
@@ -68,6 +70,10 @@
 
 def rounds_of(block):
     return [number for number, (at, _) in enumerate(ROUNDS) if at == block]
+
+
+def in_line(number, core):
+    return ROUTES[number][core][2] == Z
 
 
 def parts_of(block):
@@ -177,6 +183,7 @@
     weight_send: Any
     send_sem: Any
     recv_sem: Any
+    out_send: Any
     last_send: Any
     last_recv: Any
     give_send: Any
@@ -216,10 +223,11 @@
         half = rows // 2
 
         shapes = [(half, 512)]
-        for _ in range(ROUTES[number][2]):
+        for _ in range(3):
             tall, wide = shapes[-1]
             shapes.append((tall // 2, wide) if tall // 2 % 16 == 0 else (tall, wide // 2))
-        shapes += [shapes[-1]] * (5 - len(shapes))
+        largest = shapes[2 if in_line(number, 0) or in_line(number, 1) else 3]
+        shapes = [*shapes[:3], largest, largest]
         return Round(
             part=pltpu.VMEM((rows, 512), BF16),
             landing=[pltpu.VMEM(shape, BF16) for shape in shapes[1:]],
@@ -248,6 +256,7 @@
         weight_send=dma((10,)),
         send_sem=dma((count,)),
         recv_sem=dma((count, 5)),
+        out_send=dma((count,)),
         last_send=dma((most,)),
         last_recv=dma((most, 2)),
         give_send=dma((4,)),
@@ -273,18 +282,8 @@
     chips = ((dpx, y), (dp, ry), (dpz, y), (dpm, y))
     sides = (x, y, lax.rem(lax.div(z + 1, 2), 2))
 
-    def by_core(pair):
-        return pair[0] if pair[0] is pair[1] else jnp.where(c == 0, *pair)
-
-    def chip(number, stage):
-        if stage == 3:
-            return chips[FAR]
-        axes = [ROUTES[number][core][stage] for core in range(2)]
-        return tuple(by_core([chips[axis][i] for axis in axes]) for i in range(2))
-
-    def side(number, stage, flip=False):
-        axes = [ROUTES[number][core ^ flip][stage] for core in range(2)]
-        return by_core([sides[axis] for axis in axes])
+    between = (z == 1) | (z == 2)
+    ends = (z == 0) | (z == 3)
 
     mine = pl.ds(pl.multiple_of(c * n, 128), n)
     label_rows = n // 128
@@ -333,11 +332,11 @@
                 waited.add((block, key))
                 weight_local(block, key).wait()
 
-    def regions(number, base):
+    def regions(number, core, base):
         keep, give = [(base, rows_of(number) // 2, 0, 512)], [None]
-        for stage in range(ROUTES[number][2]):
+        for axis in ROUTES[number][core]:
             row, rows, col, cols = keep[-1]
-            bit = side(number, stage)
+            bit = sides[axis]
             if rows // 2 % 16 == 0:
                 rows = rows // 2
                 keep.append((row + bit * rows, rows, col, cols))
@@ -353,53 +352,68 @@
 
         return [at(*area) for area in keep], [area and at(*area) for area in give]
 
-    def summed(number):
-        return regions(number, c * (rows_of(number) // 2))
-
-    def message(number, kind):
+    def summed(number, core):
+        return regions(number, core, core * (rows_of(number) // 2))
+
+    def gathered(number, core):
+        return regions(number, core, 0)[0]
+
+    def landing(number, core, kind):
+        ref = rounds[number].landing[kind]
+        if kind < S3 or in_line(number, core):
+            return ref
+        rows, cols = rounds[number].landing[S2].shape
+        rows, cols = (rows // 2, cols) if rows // 2 % 16 == 0 else (rows, cols // 2)
+        return ref.at[pl.ds(0, rows), pl.ds(0, cols)]
+
+    def message(number, core, kind):
         r = rounds[number]
-        halvings = ROUTES[number][2]
         half = rows_of(number) // 2
         if kind == D2D:
-            where = (pl.ds(pl.multiple_of(other * half, 16), half), slice(None))
-            src, dst, device = r.part.at[where], r.landing[D2D], (other, dp, y)
-        elif kind <= S4:
-            keep, give = summed(number)
-            src, dst = r.part.at[give[kind] if kind <= halvings else keep[-1]], r.landing[kind]
-            device = (c, *chip(number, kind - S1))
+            where = (pl.ds(pl.multiple_of((1 - core) * half, 16), half), slice(None))
+            src, dst, device = r.part.at[where], r.landing[D2D], (1 - core, dp, y)
+        elif kind == GD and not whole:
+            src, dst, device = r.landing[D2D], outs.rounds[number].rest, (1 - core, dp, y)
         else:
-            stage = {G3: 2, G2: 1, G1: 0, G1X: 0, GD: 0}[kind]
-            where = regions(number, 0)[0][stage + 1 if whole else 0]
-            src = r.landing[D2D].at[where]
-            dst = src if kind <= G1 else outs.rounds[number].rest.at[where]
-            device = (other, dp, y) if kind == GD else (other if kind == G1X else c, *chip(number, stage))
+            axes = (*ROUTES[number][core], FAR)
+            stage = {G3: 2, G2: 1, G1: 0, G1X: 0, GD: 0}.get(kind, kind - S1)
+            last = 2 if in_line(number, core) else 3
+            if kind <= S4:
+                keep, give = summed(number, core)
+                src, dst = r.part.at[give[kind] if kind <= last else keep[last]], landing(number, core, kind)
+            else:
+                where = gathered(number, core)[min(stage + 1, last)]
+                src = r.landing[D2D].at[where]
+                dst = src if kind <= G1 else outs.rounds[number].rest.at[where]
+            place = (dp, y) if kind == GD else chips[axes[stage]]
+            device = (1 - core if kind >= G1X else core, *place)
         return pltpu.make_async_remote_copy(
-            src, dst, *semaphores(number, kind), device_id=device, device_id_type=MESH
+            src, dst, *semaphores(number, core, kind), device_id=device, device_id_type=MESH
         )
 
-    def semaphores(number, kind):
+    def semaphores(number, core, kind):
         place = rounds_of(ROUNDS[number][0]).index(number)
-        send = s.last_send.at[place] if kind == GD else s.send_sem.at[number]
+        send = s.send_sem.at[number]
+        if kind == GD:
+            send = s.last_send.at[place]
+        elif kind == G3 and whole and in_line(number, core):
+            send = s.out_send.at[number]
         if kind >= G1X:
             return send, s.last_recv.at[place, kind - G1X]
         return send, s.recv_sem.at[number, {G1: D2D, G2: S1, G3: S2}.get(kind, kind)]
 
-    latest = {}
-
-    def begin(number, kind):
-        if number in latest:
-            message(number, latest[number]).wait_send()
-        latest[number] = kind
-        message(number, kind).start()
-
-    def fold(number, kind, where, *buffer):
+    def begin(number, core, kind, before):
+        message(number, core, before).wait_send()
+        message(number, core, kind).start()
+
+    def fold(number, core, kind, where, *buffer):
         part = rounds[number].part
-        part[where] = part[where] + rounds[number].landing[kind][buffer]
-
-    def fold_and_send(number, kind):
-        keep, give = summed(number)
+        part[where] = part[where] + landing(number, core, kind)[buffer]
+
+    def fold_and_send(number, core, kind):
+        keep, give = summed(number, core)
         level = kind + 1
-        bit = side(number, kind)
+        bit = sides[ROUTES[number][core][kind]]
         rows, cols = rounds[number].landing[kind].shape
 
         def of_landing(bit):
@@ -407,77 +421,100 @@
                 return (pl.ds(pl.multiple_of(bit * (rows // 2), 16), rows // 2), slice(None))
             return (slice(None), pl.ds(pl.multiple_of(bit * (cols // 2), 128), cols // 2))
 
-        fold(number, kind, give[level], *of_landing(1 - bit))
-        begin(number, level)
-        fold(number, kind, keep[level], *of_landing(bit))
-
-    def settle(number, kind):
+        fold(number, core, kind, give[level], *of_landing(1 - bit))
+        begin(number, core, level, kind)
+        fold(number, core, kind, keep[level], *of_landing(bit))
+
+    def settle(number, core, level):
         r = rounds[number]
-        here = regions(number, 0)[0][-1]
-        r.landing[D2D][here] = r.part[summed(number)[0][-1]] + r.landing[kind][...]
-
-    def chip_step(number):
+        here = gathered(number, core)[level]
+        r.landing[D2D][here] = r.part[summed(number, core)[0][level]] + landing(number, core, S4)[...]
+
+    def chip_step(number, core):
         block = ROUNDS[number][0]
-        message(number, D2D).wait_recv()
-        settle_half(number)
-        finish(number)
-
-        pl.when(c == block)(lambda: message(number, GD).wait_recv())
-
-    def settle_half(number):
         r = rounds[number]
-        r.landing[D2D][...] = r.landing[D2D][...] + r.part[summed(number)[0][0]]
-
-    def finish(number):
+        half = rows_of(number) // 2
+        message(number, core, D2D).wait_recv()
+        r.landing[D2D][...] = r.landing[D2D][...] + r.part[core * half : (core + 1) * half, :]
+        message(number, core, D2D).wait_send()
+        if core == block:
+            message(number, 1 - core, GD).wait_recv()
+        else:
+            message(number, core, GD).start()
+
+    def step(number, core, kind):
         block = ROUNDS[number][0]
-        message(number, latest.pop(number)).wait_send()
-        if whole:
-            pl.when(c == block)(lambda: message(number, G1).start())
-            pl.when(c != block)(lambda: message(number, G1X).start())
-        pl.when(c != block)(lambda: message(number, GD).start())
-
-    def step(number, kind):
-        block = ROUNDS[number][0]
-        halvings = ROUTES[number][2]
-        if kind < G1:
-            message(number, kind).wait_recv()
-        if kind < halvings:
-            fold_and_send(number, kind)
-        elif kind < S4:
-            if kind > halvings:
-                message(number, latest.pop(number)).wait_send()
-            fold(number, kind, summed(number)[0][-1], ...)
-            begin(number, kind + 1)
-        elif kind < G1:
-            if kind == S4:
-                settle(number, kind)
-            following = G1 + 1 - halvings if kind == S4 else kind + 1
-            if following < G1:
-                begin(number, following)
+        line = in_line(number, core)
+        keep2 = summed(number, core)[0][2]
+        if line and kind in (S3, S4):
+
+            @pl.when(between)
+            def _():
+                message(number, core, kind).wait_recv()
+                if kind == S3:
+                    fold(number, core, S3, keep2, ...)
+                    begin(number, core, S4, S2)
+                else:
+                    settle(number, core, 2)
+                    message(number, core, G3).start()
+                    begin(number, core, G2, S4)
+
+        elif line and kind == G3:
+
+            @pl.when(ends)
+            def _():
+                message(number, core, G3).wait_recv()
+                begin(number, core, G2, S3)
+
+        else:
+            message(number, core, kind).wait_recv()
+            if kind == S2 and line:
+                fold(number, core, S2, keep2, ...)
+                pl.when(ends)(lambda: begin(number, core, S3, S2))
+            elif kind < S3:
+                fold_and_send(number, core, kind)
+            elif kind == S3:
+                fold(number, core, kind, summed(number, core)[0][3], ...)
+                begin(number, core, S4, S3)
+            elif kind == S4:
+                settle(number, core, 3)
+                begin(number, core, G3, S4)
+            elif kind == G3:
+                begin(number, core, G2, G3)
             else:
-                finish(number)
-        else:
-
-            @pl.when(c == block)
-            def _():
-                quarter = rows_of(number) // 4
-                theirs = side(number, 0, flip=True)
-                for kind, ref, at in (
-                    (G1, rounds[number].landing[D2D], 1 - side(number, 0)),
-                    (GD, outs.rounds[number].rest, theirs),
-                    (G1X, outs.rounds[number].rest, 1 - theirs),
-                ):
-                    ref = ref.at[pl.ds(pl.multiple_of(at * quarter, 16), quarter)]
-                    pltpu.make_async_remote_copy(
-                        ref, ref, *semaphores(number, kind), device_id=(other, dp, y), device_id_type=MESH
-                    ).wait_recv()
-
-    def wait_sends():
+                message(number, core, G2).wait_send()
+                if core == block:
+                    message(number, core, G1).start()
+                else:
+                    message(number, core, G1X).start()
+                    message(number, core, GD).start()
+
+    def gathered_all(core):
+        for number in rounds_of(core) if whole else ():
+            quarter = rows_of(number) // 4
+            theirs = sides[ROUTES[number][1 - core][0]]
+            for kind, ref, at in (
+                (G1, rounds[number].landing[D2D], 1 - sides[ROUTES[number][core][0]]),
+                (GD, outs.rounds[number].rest, theirs),
+                (G1X, outs.rounds[number].rest, 1 - theirs),
+            ):
+                ref = ref.at[pl.ds(pl.multiple_of(at * quarter, 16), quarter)]
+                pltpu.make_async_remote_copy(
+                    ref, ref, *semaphores(number, core, kind), device_id=(other, dp, y), device_id_type=MESH
+                ).wait_recv()
+
+    def wait_sends(core):
         for number, (block, _) in enumerate(ROUNDS):
             if whole:
-                pl.when(c == block)(lambda number=number: message(number, G1).wait_send())
-                pl.when(c != block)(lambda number=number: message(number, G1X).wait_send())
-            pl.when(c != block)(lambda number=number: message(number, GD).wait_send())
+                message(number, core, G1 if core == block else G1X).wait_send()
+                if in_line(number, core):
+                    pl.when(between)(lambda number=number: message(number, core, G3).wait_send())
+            if core != block:
+                message(number, core, GD).wait_send()
+
+    def on_each_core(do):
+        for core in range(2):
+            pl.when(c == core)(functools.partial(do, core))
 
     def result(i):
         src = (s.sent, s.total, s.dinput, s.r2)[i]
@@ -616,19 +653,22 @@
         elif task == GTF_0:
             store_with_bias(0, TF, nt(one.h[4][...], one.pp[512:1024, :]), 5)
         elif task == BACK_0:
+            wait_weights(0, *late)
             end_biases(0)
             theta_b = theta(0, 0)
             one.pp[0:512, :] = theta_b
             two.h[0][0:336, :] = residual(0, theta_b).astype(BF16)
         elif task == PP_1:
+            wait_weights(1, *range(10))
             gb = -(two.gb[...] * s.mask[...])
             two.gb[...] = gb
             row_sums(1, 6, gb.astype(F32))
             two.pp[0:512, :] = tn(weights[1].back[...], gb).astype(BF16)
             two.pp[512:1024, :] = nn(weights[1].fore[...], s.gh[...]).astype(BF16)
         elif task == GT_1:
-            for k in range(2):
-                store_with_bias(1, (TB, TF)[k], nt(two.h[4][...], two.pp[512 * k : 512 * (k + 1), :]), 4 + k)
+            store_with_bias(1, TB, nt(two.h[4][...], two.pp[0:512, :]), 4)
+        elif task == GTF_1:
+            store_with_bias(1, TF, nt(two.h[4][...], two.pp[512:1024, :]), 5)
         elif task in (DH4_1, DH4_0):
             block = int(task == DH4_1)
             pp, w = blocks[block].pp, weights[block]
@@ -694,14 +734,14 @@
                 for key in keys:
                     weight_remote(block, key).start()
 
+    loads.look.start()
+    loads.past.start()
     barrier = pltpu.get_barrier_semaphore()
     greeted = [(other, dp, y)]
     if whole:
         greeted += [(c, *place) for place in chips] + [(other, *place) for place in chips[:FAR]]
     for device in greeted:
         pl.semaphore_signal(barrier, inc=1, device_id=device, device_id_type=MESH)
-    loads.look.start()
-    loads.past.start()
     fetch(names.first, names.hid, names.mid0)
     pl.semaphore_wait(barrier, len(greeted))
     send_weights(names.first, names.hid, names.mid0)
@@ -721,14 +761,16 @@
             for number in range(len(ROUNDS)):
                 if not missing[number] and number not in sent:
                     sent.add(number)
-                    begin(number, D2D)
+                    message(number, c, D2D).start()
         elif whole:
-            step((item - STEP) // 10, (item - STEP) % 10)
+            number, kind = (item - STEP) // 10, (item - STEP) % 10
+            on_each_core(lambda core: step(number, core, kind))
     if not whole:
         for number in range(len(ROUNDS)):
-            chip_step(number)
-
-    wait_sends()
+            on_each_core(lambda core: chip_step(number, core))
+
+    on_each_core(gathered_all)
+    on_each_core(wait_sends)
     for key in range(10):
         for block in range(2):
             pl.when(c == block)(lambda block=block, key=key: weight_remote(block, key).wait_send())
@@ -750,10 +792,12 @@
 
 def widen(treedef, *refs):
     held, outs, wide, sem = jax.tree.unflatten(treedef, refs)
-    names = Final(*range(10))
-
-    def leaving(i):
-        return pltpu.make_async_copy(wide[i], outs[i], sem.at[i])
+    leaving = []
+
+    def leave(ref, out):
+        copy = pltpu.make_async_copy(ref, out, sem.at[len(leaving)])
+        copy.start()
+        leaving.append(copy)
 
     def take(block):
         parts = parts_of(block)
@@ -761,12 +805,19 @@
             number, core, low, count, piece, first = part
             source = held.rounds[number].own if core == block else held.rounds[number].rest
             rows = source[low : low + count, :].astype(F32)
+            ref, out = (
+                (wide.back, outs.back),
+                (wide.fore, outs.fore),
+                *((wide.theta.at[k], outs.theta.at[k]) for k in range(2)),
+                *((wide.mid.at[k], outs.mid.at[k]) for k in range(3)),
+                (wide.first, outs.first),
+            )[piece]
             if piece == FORE:
                 k = int(parts[i - 1] == part)
-                wide.fore[256 * k + first : 256 * k + first + count, :] = rows[:, 256 * k : 256 * (k + 1)]
+                ref[256 * k + first : 256 * k + first + count, :] = rows[:, 256 * k : 256 * (k + 1)]
             elif piece == FIRST:
                 used = min(count, 336 - first)
-                wide.first[first : first + used, :] = rows[:used]
+                ref[first : first + used, :] = rows[:used]
                 if used < count:
                     lines = rows[used : used + 8]
                     for k in range(24):
@@ -774,24 +825,28 @@
                         wide.hid[k : k + 1, :] = lines[k // 4 : k // 4 + 1, at : at + 128]
                     wide.backb[...] = lines[6:7, 0:336]
                     wide.foreb[...] = lines[7:8, 0:256]
-            elif piece == BACK:
-                wide.back[first : first + count, :] = rows
-            elif piece in (TB, TF):
-                wide.theta[piece - TB, first : first + count, :] = rows
+                    for one, two in ((wide.hid, outs.hid), (wide.backb, outs.backb), (wide.foreb, outs.foreb)):
+                        leave(one, two)
             else:
-                wide.mid[piece - M0, first : first + count, :] = rows
-
-    wide.outcome[...] = held.outcome[...].astype(F32)
-    leaving(names.outcome).start()
-    wide.pair[...] = held.pair[...].astype(F32)
-    leaving(names.pair).start()
+                ref[first : first + count, :] = rows
+            if not any(later[4] == piece for later in parts[i + 1 :]):
+                leave(ref, out)
+
+    def all_of(block):
+        leaving.clear()
+        for k in range(3):
+            some = pl.ds(112 * k, 112)
+            wide.outcome[some, :] = held.outcome[some, :].astype(F32)
+            leave(wide.outcome.at[some], outs.outcome.at[some])
+        wide.pair[...] = held.pair[...].astype(F32)
+        leave(wide.pair, outs.pair)
+        take(block)
+        for copy in leaving:
+            copy.wait()
+
     c = lax.axis_index("section")
     for block in range(2):
-        pl.when(c == block)(functools.partial(take, block))
-    for i in range(2, 10):
-        leaving(i).start()
-    for i in range(10):
-        leaving(i).wait()
+        pl.when(c == block)(functools.partial(all_of, block))
 
 
 def shards(whole, past, label, look, scored, adjp, adjl, first, mid, theta, back, fore, hid, backb, foreb):
@@ -837,7 +892,7 @@
     )
     final = Final(*(shape(dims, F32) for dims in shapes))
     wide = Final(*(pltpu.VMEM(dims, F32) for dims in shapes))
-    sem = pltpu.SemaphoreType.DMA((10,))
+    sem = pltpu.SemaphoreType.DMA((15,))
     treedef = jax.tree.structure((results, final, wide, sem))
     final = pl.pallas_call(
         functools.partial(widen, treedef),

time: 87.5 us -> 86.2 us (0.985)
  Pallas kernels: 86.5 us -> 85.2 us
    pallas_call x1, Pallas kernels: 82.2 us -> 81 us  [shards(): pl.pallas_call(functools.partial(body, n, whole, treedef), out_shape=plac...]
where the time goes in v3:
time: 86.2 us; the launch traced here: 86 us
  Pallas kernels  85.2 us (99%)
    pallas_call x1, Pallas kernels, shards(): pl.pallas_call(functools.partial(body, n, whole, treedef), out_shape=plac...  81 us
    pallas_call x1, Pallas kernels, shards(): pl.pallas_call(functools.partial(widen, treedef), out_shape=final, in_spe...  4.16 us

profile of v3, /device:TPU:0, one launch (start us, length us, event | category | flops | bytes accessed | tf_op | source)
XLA Modules:
  0.0 86.0 jit_solution(14003118461410156063)
XLA Ops:
  0.6 81.0 %shard_map.213 = (bf16[64,2048]{1,0:T(8,128)(2,1)S(1)}, bf16[336,2048]{1,0:T(8,128)(2,1)S(1)}, bf16[256,512]{1,0:T(8,128)(2,1)S(1)}, bf16[256,512]{1,0:T(8,128)(...) custom-call(bf16[336,2048]{1,0:T(8,128)(2,1)} %bitcast.25, ...), custom_call_target="tpu_custom_call" | custom-call | tf_op jit(solution)/shard_map/pallas_call | solution.py:870
  81.7 4.2 %shard_map.214 = (f32[64,2048]{1,0:T(8,128)}, f32[336,2048]{1,0:T(8,128)}, f32[336,512]{1,0:T(8,128)}, f32[3,512,512]{2,1,0:T(8,128)}, f32[2,512,512]{2,1,0:T(8,...) custom-call(bf16[64,2048]{1,0:T(8,128)(2,1)S(1)} %get-tuple-element., ...), custom_call_target="tpu_custom_call" | custom-call | tf_op jit(solution)/shard_map/pallas_call | solution.py:897

commit v4 on v3

--- a/solution.py
+++ b/solution.py
@@ -140,7 +140,8 @@
     mid0: Any
     mid1: Any
     mid2: Any
-    theta: Any
+    theta_b: Any
+    theta_f: Any
     back: Any
     backb: Any
     fore: Any
@@ -199,7 +200,8 @@
             mid0=square,
             mid1=square,
             mid2=square,
-            theta=pltpu.VMEM((2, 512, 512), BF16),
+            theta_b=square,
+            theta_f=square,
             back=pltpu.VMEM((336, 512), BF16),
             backb=pltpu.VMEM((1, 336), F32),
             fore=pltpu.VMEM((512, 256), BF16),
@@ -252,8 +254,8 @@
         dinput=pltpu.VMEM((336, n), BF16),
         r2=pltpu.VMEM((336, n), BF16),
         load_sem=dma((6,)),
-        weight_sem=dma((2, 10)),
-        weight_send=dma((10,)),
+        weight_sem=dma((2, 11)),
+        weight_send=dma((11,)),
         send_sem=dma((count,)),
         recv_sem=dma((count, 5)),
         out_send=dma((count,)),
@@ -302,7 +304,8 @@
         mid0=given.mid.at[0, 0],
         mid1=given.mid.at[0, 1],
         mid2=given.mid.at[0, 2],
-        theta=given.theta.at[0],
+        theta_b=given.theta.at[0, 0],
+        theta_f=given.theta.at[0, 1],
         back=given.back,
         backb=given.backb,
         fore=given.fore.at[0],
@@ -322,7 +325,7 @@
             device_id_type=MESH,
         )
 
-    names = Weights(*range(10))
+    names = Weights(*range(11))
 
     waited = set()
 
@@ -577,7 +580,7 @@
         b.d[depth - 1][...] = (sig + out * (1.0 - sig)).astype(BF16)
 
     def theta(block, k):
-        return (tn(weights[block].theta[k], blocks[block].h[4][0:512, :]) + blocks[block].hid[:, 4 + k : 5 + k]).astype(BF16)
+        return (tn(weights[block][names.theta_b + k][...], blocks[block].h[4][0:512, :]) + blocks[block].hid[:, 4 + k : 5 + k]).astype(BF16)
 
     def heads(block, theta_f):
         wide = tn(weights[block].fore[...], theta_f) + blocks[block].foreb[:, 0:1]
@@ -623,19 +626,16 @@
             layer_biases(0)
         elif task in (Z1_0, Z2_0, Z3_0, Z4_0):
             depth = task - Z1_0 + 1
-            if depth == 1:
-                wait_weights(0, names.first, names.mid0)
-            elif depth == 3:
-                wait_weights(0, names.mid1, names.mid2)
+            wait_weights(0, (names.first, names.mid0, names.mid1, names.mid2)[depth - 1])
             layer(0, depth)
         elif task in (Z1_1, Z2_1, Z3_1, Z4_1):
             depth = task - Z1_1 + 1
             if depth == 1:
-                wait_weights(1, *range(10))
+                wait_weights(1, *range(11))
                 layer_biases(1)
             layer(1, depth)
         elif task == GH_0:
-            wait_weights(0, *late)
+            wait_weights(0, names.fore)
             for load in (loads.label, loads.scored, loads.adjp, loads.adjl):
                 load.wait()
             for b in blocks:
@@ -653,13 +653,13 @@
         elif task == GTF_0:
             store_with_bias(0, TF, nt(one.h[4][...], one.pp[512:1024, :]), 5)
         elif task == BACK_0:
-            wait_weights(0, *late)
+            wait_weights(0, *late[:-1])
             end_biases(0)
             theta_b = theta(0, 0)
             one.pp[0:512, :] = theta_b
             two.h[0][0:336, :] = residual(0, theta_b).astype(BF16)
         elif task == PP_1:
-            wait_weights(1, *range(10))
+            wait_weights(1, *range(11))
             gb = -(two.gb[...] * s.mask[...])
             two.gb[...] = gb
             row_sums(1, 6, gb.astype(F32))
@@ -671,8 +671,9 @@
             store_with_bias(1, TF, nt(two.h[4][...], two.pp[512:1024, :]), 5)
         elif task in (DH4_1, DH4_0):
             block = int(task == DH4_1)
+            wait_weights(block, names.theta_f)
             pp, w = blocks[block].pp, weights[block]
-            inward(block, 4, nn(w.theta[0], pp[0:512, :]) + nn(w.theta[1], pp[512:1024, :]))
+            inward(block, 4, nn(w.theta_b[...], pp[0:512, :]) + nn(w.theta_f[...], pp[512:1024, :]))
         elif task in (B3_1, B2_1, B1_1, B3_0, B2_0, B1_0):
             block = int(task < GB_0)
             depth = 4 - (task - (B3_1 if block else B3_0))
@@ -702,6 +703,7 @@
         elif task == GTB_0:
             store_with_bias(0, TB, nt(one.h[4][...], one.pp[0:512, :]), 4)
         elif task == HEADS_0:
+            wait_weights(0, names.theta_f)
             theta_f = theta(0, 1)
             store(0, FORE, nt(theta_f, s.gh[...]))
             s.sent[...] = heads(0, theta_f).astype(BF16)
@@ -726,13 +728,11 @@
                 for key in keys:
                     weight_local(block, key).start()
 
-    def send_weights(*keys):
-        for block in range(2):
-
-            @pl.when(c == block)
-            def _(block=block):
-                for key in keys:
-                    weight_remote(block, key).start()
+    def send_weights(block, *keys):
+        @pl.when(c == block)
+        def _():
+            for key in keys:
+                weight_remote(block, key).start()
 
     loads.look.start()
     loads.past.start()
@@ -744,18 +744,19 @@
         pl.semaphore_signal(barrier, inc=1, device_id=device, device_id_type=MESH)
     fetch(names.first, names.hid, names.mid0)
     pl.semaphore_wait(barrier, len(greeted))
-    send_weights(names.first, names.hid, names.mid0)
-    late = (names.fore, names.theta, names.back, names.backb, names.foreb)
-    after = {LOAD: ((names.mid1, names.mid2, *late), (names.mid1, names.mid2)), Z2_0: ((), late)}
+    late = (names.fore, names.theta_b, names.back, names.backb, names.foreb, names.theta_f)
+    send_weights(0, names.first, names.hid, names.mid0)
+    send_weights(1, names.first, names.hid, names.mid0, names.mid1, names.mid2, *late)
+    after = {LOAD: (names.mid1, names.mid2), Z2_0: late[:2], Z3_0: late[2:]}
 
     sent = set()
     for item in ORDER:
         if item < STEP:
             run(item)
             if item in after:
-                fetch(*after[item][0])
-                send_weights(*after[item][1])
+                send_weights(0, *after[item])
             if item == LOAD:
+                fetch(names.mid1, names.mid2, *late)
                 for load in (loads.label, loads.scored, loads.adjp, loads.adjl):
                     load.start()
             for number in range(len(ROUNDS)):
@@ -771,7 +772,7 @@
 
     on_each_core(gathered_all)
     on_each_core(wait_sends)
-    for key in range(10):
+    for key in range(11):
         for block in range(2):
             pl.when(c == block)(lambda block=block, key=key: weight_remote(block, key).wait_send())
     handed_over()

time: 86.2 us -> 85.4 us (level)
  no operation moved by 1% of the time
where the time goes in v4:
time: 85.4 us; the launch traced here: 85.3 us
  Pallas kernels  84.4 us (99%)
    pallas_call x1, Pallas kernels, shards(): pl.pallas_call(functools.partial(body, n, whole, treedef), out_shape=plac...  80.3 us
    pallas_call x1, Pallas kernels, shards(): pl.pallas_call(functools.partial(widen, treedef), out_shape=final, in_spe...  4.16 us

profile of v4, /device:TPU:0, one launch (start us, length us, event | category | flops | bytes accessed | tf_op | source)
XLA Modules:
  0.0 85.3 jit_solution(4990392693462068872)
XLA Ops:
  0.6 80.3 %shard_map.213 = (bf16[64,2048]{1,0:T(8,128)(2,1)S(1)}, bf16[336,2048]{1,0:T(8,128)(2,1)S(1)}, bf16[256,512]{1,0:T(8,128)(2,1)S(1)}, bf16[256,512]{1,0:T(8,128)(...) custom-call(bf16[336,2048]{1,0:T(8,128)(2,1)} %bitcast.25, ...), custom_call_target="tpu_custom_call" | custom-call | tf_op jit(solution)/shard_map/pallas_call | solution.py:871
  80.9 4.2 %shard_map.214 = (f32[64,2048]{1,0:T(8,128)}, f32[336,2048]{1,0:T(8,128)}, f32[336,512]{1,0:T(8,128)}, f32[3,512,512]{2,1,0:T(8,128)}, f32[2,512,512]{2,1,0:T(8,...) custom-call(bf16[64,2048]{1,0:T(8,128)(2,1)S(1)} %get-tuple-element., ...), custom_call_target="tpu_custom_call" | custom-call | tf_op jit(solution)/shard_map/pallas_call | solution.py:898

commit v5 on v4

--- a/solution.py
+++ b/solution.py
@@ -742,11 +742,11 @@
         greeted += [(c, *place) for place in chips] + [(other, *place) for place in chips[:FAR]]
     for device in greeted:
         pl.semaphore_signal(barrier, inc=1, device_id=device, device_id_type=MESH)
-    fetch(names.first, names.hid, names.mid0)
     pl.semaphore_wait(barrier, len(greeted))
     late = (names.fore, names.theta_b, names.back, names.backb, names.foreb, names.theta_f)
     send_weights(0, names.first, names.hid, names.mid0)
-    send_weights(1, names.first, names.hid, names.mid0, names.mid1, names.mid2, *late)
+    fetch(names.first, names.hid, names.mid0)
+    send_weights(1, names.first, names.hid, names.mid0, names.mid1, names.mid2)
     after = {LOAD: (names.mid1, names.mid2), Z2_0: late[:2], Z3_0: late[2:]}
 
     sent = set()
@@ -757,6 +757,7 @@
                 send_weights(0, *after[item])
             if item == LOAD:
                 fetch(names.mid1, names.mid2, *late)
+                send_weights(1, *late)
                 for load in (loads.label, loads.scored, loads.adjp, loads.adjl):
                     load.start()
             for number in range(len(ROUNDS)):

time: 85.4 us -> 85.8 us (level)
  no operation moved by 1% of the time
where the time goes in v5:
time: 85.8 us; the launch traced here: 85.6 us
  Pallas kernels  84.8 us (99%)
    pallas_call x1, Pallas kernels, shards(): pl.pallas_call(functools.partial(body, n, whole, treedef), out_shape=plac...  80.6 us
    pallas_call x1, Pallas kernels, shards(): pl.pallas_call(functools.partial(widen, treedef), out_shape=final, in_spe...  4.16 us

profile of v5, /device:TPU:0, one launch (start us, length us, event | category | flops | bytes accessed | tf_op | source)
XLA Modules:
  0.0 85.6 jit_solution(2169142799913571259)
XLA Ops:
  0.6 80.6 %shard_map.213 = (bf16[64,2048]{1,0:T(8,128)(2,1)S(1)}, bf16[336,2048]{1,0:T(8,128)(2,1)S(1)}, bf16[256,512]{1,0:T(8,128)(2,1)S(1)}, bf16[256,512]{1,0:T(8,128)(...) custom-call(bf16[336,2048]{1,0:T(8,128)(2,1)} %bitcast.25, ...), custom_call_target="tpu_custom_call" | custom-call | tf_op jit(solution)/shard_map/pallas_call | solution.py:872
  81.3 4.2 %shard_map.214 = (f32[64,2048]{1,0:T(8,128)}, f32[336,2048]{1,0:T(8,128)}, f32[336,512]{1,0:T(8,128)}, f32[3,512,512]{2,1,0:T(8,128)}, f32[2,512,512]{2,1,0:T(8,...) custom-call(bf16[64,2048]{1,0:T(8,128)(2,1)S(1)} %get-tuple-element., ...), custom_call_target="tpu_custom_call" | custom-call | tf_op jit(solution)/shard_map/pallas_call | solution.py:899
